TPU v7x, 32 devices: a whole 2x2x4 slice. The times are simulated.
32 devices in a mesh: seq: 8 (over z, y), grp: 4 (over x, core).
Axes of the slice: x: 2, y: 2, z: 4, core: 2. Of those that a mesh axis runs over, the one named last changes fastest.
Arguments:
- pre_x: bfloat16 [4096, 16384], P('seq', 'grp'), may hold values from -6 to 6
- pre_b: bfloat16 [4096, 2048], P('seq'), may hold values from -6 to 6
- pre_c: bfloat16 [4096, 2048], P('seq'), may hold values from -6 to 6
- pre_dt: float32 [256, 4096], P('grp', 'seq'), may hold values from 0.004 to 0.016
- decay_rate: float32 [256], replicated, may hold values from 0.0078125 to 5
- skip_gain: float32 [256], replicated, may hold values from 0.5 to 1.5
- conv_taps: float32 [4, 20480], replicated, may hold values from -3 to 3
- dec_x: bfloat16 [2, 32, 16384], P(None, 'grp', 'seq'), may hold values from -6 to 6
- dec_b: bfloat16 [2, 32, 2048], P(None, 'grp'), may hold values from -6 to 6
- dec_c: bfloat16 [2, 32, 2048], P(None, 'grp'), may hold values from -6 to 6
- dec_dt: float32 [2, 32, 256], P(None, 'grp', 'seq'), may hold values from 0.004 to 0.016
- dec_query: bfloat16 [2, 32, 8192], P(None, 'grp'), may hold values from -12 to 12
- new_kv: bfloat16 [2, 2, 32, 1024], P(None, None, 'grp'), may hold values from -6 to 6
- cache_kv: bfloat16 [2, 32, 512, 1024], P(None, 'grp', 'seq'), may hold values from -12 to 12
- kv_len: int32 [32], P('grp'), may hold values from 2 to 512, as said below
Outputs:
- pre_y: bfloat16 [4096, 16384], P('seq', 'grp')
- dec_y: bfloat16 [2, 32, 16384], P(None, 'grp', 'seq')
- attn_out: bfloat16 [2, 32, 8192], P(None, 'grp', 'seq')
Inputs may be any that keep to these rules, and one draw needn't show every extreme that they name: `kv_len`: row 0 of every group of 8 rows has all 512 positions valid.
All inputs are finite; a program needn't handle non-finite values.
Results may differ from a plain program's by a relative error of at most 0.0013.
Values sent between devices are 32-bit elements; how exact they have to be, the bound alone decides.
A program may use at most 128 MiB of HBM per device.

v0:
```python
import jax
import jax.numpy as jnp
from jax import lax
from jax.sharding import PartitionSpec as P

HEADS = 256
HDIM = 64
STATE = 256
GROUPS = 8
TAPS = 4
QHEADS = 64
KVHEADS = 8
ADIM = 128
SPAN = 256
STEPS = 2


HIGH = lax.Precision.HIGHEST
NEG = -1e30


def passed_along(value, axis, steps):
    count = lax.axis_size(axis)
    first, last = (max(0, -steps), min(count, count - steps))
    return lax.ppermute(value, axis, [(source, source + steps) for source in range(first, last)])


def from_root(value, axis, source):
    kept = jnp.where(lax.axis_index(axis) == source, value, 0).astype(value.dtype)
    return lax.psum(kept, axis)


def causal_conv(leading, source, kernel):
    row_total = source.shape[0]
    padded = jnp.concatenate([leading, source], axis=0)
    accumulated = jnp.zeros_like(source)
    for position in range(TAPS):
        accumulated = accumulated + kernel[position] * padded[position : position + row_total]
    return jax.nn.silu(accumulated)


def decode_conv(leading, fresh, kernel):
    results = []
    for current in range(fresh.shape[0]):
        accumulated = jnp.zeros(fresh.shape[1:], jnp.float32)
        for position in range(TAPS):
            place = current + position
            if place < TAPS - 1:
                term = leading[place][None, :]
            else:
                term = fresh[place - (TAPS - 1)]
            accumulated = accumulated + kernel[position] * term
        results.append(jax.nn.silu(accumulated))
    return jnp.stack(results)


def span_pass(ssm_state, block):
    inputs, entries, readout, log_decay = block
    cumulative = jnp.cumsum(log_decay, axis=1)
    block_size = log_decay.shape[1]
    causal = jnp.arange(block_size)[:, None] >= jnp.arange(block_size)[None, :]
    spreads = cumulative[:, :, None] - cumulative[:, None, :]
    weights = jnp.where(causal[None], jnp.exp(jnp.where(causal[None], spreads, 0.0)), 0.0)
    intersection = jnp.dot(readout, entries.T, precision=HIGH)
    intra_span = jnp.einsum("kts,skp->tkp", weights * intersection[None], inputs, precision=HIGH)
    carried = jnp.exp(cumulative).T[:, :, None] * jnp.einsum(
        "tn,kpn->tkp", readout, ssm_state, precision=HIGH
    )
    remaining = jnp.exp(cumulative[:, -1:] - cumulative)
    updates = jnp.einsum("skp,sn->kpn", inputs * remaining.T[:, :, None], entries, precision=HIGH)
    renewed = jnp.exp(cumulative[:, -1])[:, None, None] * ssm_state + updates
    return (renewed, intra_span + carried)


def run_spans(inputs, entries, readout, log_decay, ssm_state):
    row_total, heads_here, head_width = inputs.shape
    block_total = row_total // SPAN
    blocks = (
        inputs.reshape(block_total, SPAN, heads_here, head_width),
        entries.reshape(block_total, SPAN, entries.shape[1]),
        readout.reshape(block_total, SPAN, readout.shape[1]),
        log_decay.reshape(heads_here, block_total, SPAN).transpose(1, 0, 2),
    )
    ssm_state, results = lax.scan(span_pass, ssm_state, blocks)
    return (results.reshape(row_total, heads_here, head_width), ssm_state)


def decode_mamba(ssm_state, heads_x, heads_b, heads_c, step_dt, rates, gains):
    decays = jnp.exp(-step_dt * rates)
    from_prefix = jnp.einsum("jrhn,hpn->jrhp", heads_c, ssm_state, precision=HIGH)
    results = []
    for current in range(heads_x.shape[0]):
        factor = jnp.ones(decays.shape[1:], jnp.float32)
        accumulated = gains[None, :, None] * heads_x[current]
        for earlier in range(current, -1, -1):
            intersection = jnp.sum(heads_c[current] * heads_b[earlier], axis=-1)
            accumulated = (
                accumulated
                + (factor * step_dt[earlier] * intersection)[..., None] * heads_x[earlier]
            )
            factor = factor * decays[earlier]
        accumulated = accumulated + factor[..., None] * from_prefix[current]
        results.append(accumulated)
    return jnp.stack(results)


def group_layout(head_begin, head_count):
    per_group = HEADS // GROUPS
    group_count = max(1, head_count // per_group)
    return (head_begin // per_group, group_count, head_count // group_count)


def on_device(
    pre_x,
    pre_b,
    pre_c,
    pre_dt,
    decay_rate,
    skip_gain,
    conv_taps,
    dec_x,
    dec_b,
    dec_c,
    dec_dt,
    dec_query,
    new_kv,
    cache_kv,
    kv_len,
):
    seq_count = lax.axis_size("seq")
    seq_index = lax.axis_index("seq")
    grp_index = lax.axis_index("grp")
    section = pre_x.shape[0]
    local_heads = pre_x.shape[1] // HDIM
    edge = TAPS - 1
    x_offset = HEADS * HDIM
    c_offset = HEADS * HDIM + GROUPS * STATE
    head_begin = grp_index * local_heads
    group_begin, group_count, heads_each = group_layout(head_begin, local_heads)
    source_x = pre_x.astype(jnp.float32)
    full_b = pre_b.astype(jnp.float32)
    full_c = pre_c.astype(jnp.float32)
    tail_rows = (source_x[section - edge :], full_b[section - edge :], full_c[section - edge :])
    leading = passed_along((tail_rows[0], tail_rows[1], tail_rows[2]), "seq", 1)
    kernel_x = lax.dynamic_slice_in_dim(conv_taps, head_begin * HDIM, local_heads * HDIM, 1)
    kernel_b = lax.dynamic_slice_in_dim(
        conv_taps, x_offset + group_begin * STATE, group_count * STATE, 1
    )
    kernel_c = lax.dynamic_slice_in_dim(
        conv_taps, c_offset + group_begin * STATE, group_count * STATE, 1
    )
    conv_x = causal_conv(leading[0], source_x, kernel_x)
    conv_b = causal_conv(
        lax.dynamic_slice_in_dim(leading[1], group_begin * STATE, group_count * STATE, 1),
        lax.dynamic_slice_in_dim(full_b, group_begin * STATE, group_count * STATE, 1),
        kernel_b,
    )
    conv_c = causal_conv(
        lax.dynamic_slice_in_dim(leading[2], group_begin * STATE, group_count * STATE, 1),
        lax.dynamic_slice_in_dim(full_c, group_begin * STATE, group_count * STATE, 1),
        kernel_c,
    )
    rates = lax.dynamic_slice_in_dim(decay_rate, head_begin, local_heads, 0)
    gains = lax.dynamic_slice_in_dim(skip_gain, head_begin, local_heads, 0)
    log_decay = -pre_dt * rates[:, None]
    head_inputs = conv_x.reshape(section, local_heads, HDIM)
    scaled = head_inputs * pre_dt.T[:, :, None]
    grouped = scaled.reshape(section, group_count, heads_each, HDIM).transpose(1, 0, 2, 3)
    entries = conv_b.reshape(section, group_count, STATE).transpose(1, 0, 2)
    readout = conv_c.reshape(section, group_count, STATE).transpose(1, 0, 2)
    decay_groups = log_decay.reshape(group_count, heads_each, section)
    blank = jnp.zeros((group_count, heads_each, HDIM, STATE), jnp.float32)
    intra_part, closing_local = jax.vmap(run_spans)(grouped, entries, readout, decay_groups, blank)
    local_state = closing_local.reshape(local_heads, HDIM, STATE)
    cumulative = jnp.cumsum(log_decay, axis=1)
    section_decay = cumulative[:, -1]

    def relay(counter, arriving):
        leaving = jnp.exp(section_decay)[:, None, None] * arriving + local_state
        return passed_along(leaving, "seq", 1)

    incoming = lax.fori_loop(0, seq_count - 1, relay, jnp.zeros_like(local_state))
    incoming_groups = incoming.reshape(group_count, heads_each, HDIM, STATE)
    from_before = jnp.einsum("gsn,gkpn->gskp", readout, incoming_groups, precision=HIGH)
    decay_factor = jnp.exp(cumulative).reshape(group_count, heads_each, section).transpose(0, 2, 1)
    combined = intra_part + decay_factor[..., None] * from_before
    combined = (
        combined.transpose(1, 0, 2, 3).reshape(section, local_heads, HDIM)
        + gains[None, :, None] * head_inputs
    )
    pre_y = combined.reshape(section, local_heads * HDIM).astype(jnp.bfloat16)
    closing = jnp.exp(section_decay)[:, None, None] * incoming + local_state
    final_state, tail_x, tail_b, tail_c = (
        from_root(closing, "seq", seq_count - 1),
        from_root(tail_rows[0], "seq", seq_count - 1),
        from_root(tail_rows[1], "seq", seq_count - 1),
        from_root(tail_rows[2], "seq", seq_count - 1),
    )
    state_heads = HEADS // seq_count
    root_group = seq_index * state_heads // local_heads
    offset_heads = seq_index * state_heads - root_group * local_heads
    own_state = lax.dynamic_slice_in_dim(final_state, offset_heads, state_heads, 0)
    own_tail = lax.dynamic_slice_in_dim(tail_x, offset_heads * HDIM, state_heads * HDIM, 1)
    prefix_state, prefix_tail = (
        from_root(own_state, "grp", root_group),
        from_root(own_tail, "grp", root_group),
    )
    rows_here = dec_x.shape[1]
    dec_begin = seq_index * state_heads
    dgroup_begin, dgroup_count, dheads_each = group_layout(dec_begin, state_heads)
    kernel_dx = lax.dynamic_slice_in_dim(conv_taps, dec_begin * HDIM, state_heads * HDIM, 1)
    kernel_db = lax.dynamic_slice_in_dim(
        conv_taps, x_offset + dgroup_begin * STATE, dgroup_count * STATE, 1
    )
    kernel_dc = lax.dynamic_slice_in_dim(
        conv_taps, c_offset + dgroup_begin * STATE, dgroup_count * STATE, 1
    )
    step_x = decode_conv(prefix_tail, dec_x.astype(jnp.float32), kernel_dx)
    step_b = decode_conv(
        lax.dynamic_slice_in_dim(tail_b, dgroup_begin * STATE, dgroup_count * STATE, 1),
        lax.dynamic_slice_in_dim(dec_b, dgroup_begin * STATE, dgroup_count * STATE, 2).astype(
            jnp.float32
        ),
        kernel_db,
    )
    step_c = decode_conv(
        lax.dynamic_slice_in_dim(tail_c, dgroup_begin * STATE, dgroup_count * STATE, 1),
        lax.dynamic_slice_in_dim(dec_c, dgroup_begin * STATE, dgroup_count * STATE, 2).astype(
            jnp.float32
        ),
        kernel_dc,
    )
    heads_x = step_x.reshape(STEPS, rows_here, state_heads, HDIM)
    heads_b = jnp.repeat(step_b.reshape(STEPS, rows_here, dgroup_count, STATE), dheads_each, axis=2)
    heads_c = jnp.repeat(step_c.reshape(STEPS, rows_here, dgroup_count, STATE), dheads_each, axis=2)
    dec_rates = lax.dynamic_slice_in_dim(decay_rate, dec_begin, state_heads, 0)
    dec_gains = lax.dynamic_slice_in_dim(skip_gain, dec_begin, state_heads, 0)
    mamba_out = decode_mamba(prefix_state, heads_x, heads_b, heads_c, dec_dt, dec_rates, dec_gains)
    dec_y = mamba_out.reshape(STEPS, rows_here, state_heads * HDIM).astype(jnp.bfloat16)
    group_size = QHEADS // KVHEADS
    score_scale = ADIM ** (-0.5)
    positions = cache_kv.shape[2]
    queries = dec_query.reshape(STEPS, rows_here, KVHEADS, group_size, ADIM)
    key_rows = cache_kv[0].reshape(rows_here, positions, KVHEADS, ADIM)
    value_rows = cache_kv[1].reshape(rows_here, positions, KVHEADS, ADIM).astype(jnp.float32)
    scores = (
        jnp.einsum("jrkgd,rckd->jrkgc", queries, key_rows, preferred_element_type=jnp.float32)
        * score_scale
    )
    places = seq_index * positions + jnp.arange(positions)
    usable = (places[None, :] < kv_len[:, None])[None, :, None, None, :]
    scores = jnp.where(usable, scores, NEG)
    peak_local = jnp.max(scores, axis=-1)
    weights = jnp.where(usable, jnp.exp(scores - peak_local[..., None]), 0.0)
    mass_local = jnp.sum(weights, axis=-1)
    summed_local = jnp.einsum("jrkgc,rckd->jrkgd", weights, value_rows, precision=HIGH)
    peak_local = peak_local.reshape(STEPS, rows_here, QHEADS)
    mass_local = mass_local.reshape(STEPS, rows_here, QHEADS)
    summed_local = summed_local.reshape(STEPS, rows_here, QHEADS, ADIM)
    own_heads = QHEADS // seq_count
    head_start = seq_index * own_heads
    pieces = (
        lax.all_to_all(peak_local[None], "seq", split_axis=3, concat_axis=0, tiled=True),
        lax.all_to_all(mass_local[None], "seq", split_axis=3, concat_axis=0, tiled=True),
        lax.all_to_all(summed_local[None], "seq", split_axis=3, concat_axis=0, tiled=True),
    )
    peak_cache = jnp.max(pieces[0], axis=0)
    rescale = jnp.exp(pieces[0] - peak_cache[None])
    mass_cache = jnp.sum(pieces[1] * rescale, axis=0)
    summed_cache = jnp.sum(pieces[2] * rescale[..., None], axis=0)
    new_keys = new_kv[0].reshape(STEPS, rows_here, KVHEADS, ADIM)
    new_values = new_kv[1].reshape(STEPS, rows_here, KVHEADS, ADIM).astype(jnp.float32)
    new_scores = (
        jnp.einsum("jrkgd,irkd->jrkgi", queries, new_keys, preferred_element_type=jnp.float32)
        * score_scale
    )
    allowed = (jnp.arange(STEPS)[None, :] <= jnp.arange(STEPS)[:, None])[:, None, None, None, :]
    new_scores = jnp.where(allowed, new_scores, NEG)
    new_scores = lax.dynamic_slice_in_dim(
        new_scores.reshape(STEPS, rows_here, QHEADS, STEPS), head_start, own_heads, 2
    )
    allowed_heads = (jnp.arange(STEPS)[None, :] <= jnp.arange(STEPS)[:, None])[:, None, None, :]
    head_kv = (head_start + jnp.arange(own_heads)) // group_size
    pick = (head_kv[:, None] == jnp.arange(KVHEADS)[None, :]).astype(jnp.float32)
    own_values = jnp.einsum("hk,irkd->irhd", pick, new_values, precision=HIGH)
    peak_total = jnp.maximum(peak_cache, jnp.max(new_scores, axis=-1))
    cache_scale = jnp.exp(peak_cache - peak_total)
    new_weights = jnp.where(allowed_heads, jnp.exp(new_scores - peak_total[..., None]), 0.0)
    mass_total = mass_cache * cache_scale + jnp.sum(new_weights, axis=-1)
    summed_total = summed_cache * cache_scale[..., None] + jnp.einsum(
        "jrhi,irhd->jrhd", new_weights, own_values, precision=HIGH
    )
    attn_out = (
        (summed_total / mass_total[..., None])
        .reshape(STEPS, rows_here, own_heads * ADIM)
        .astype(jnp.bfloat16)
    )
    return (pre_y, dec_y, attn_out)


def solution(mesh):
    in_specs = (
        P("seq", "grp"),
        P("seq", None),
        P("seq", None),
        P("grp", "seq"),
        P(),
        P(),
        P(),
        P(None, "grp", "seq"),
        P(None, "grp", None),
        P(None, "grp", None),
        P(None, "grp", "seq"),
        P(None, "grp", None),
        P(None, None, "grp", None),
        P(None, "grp", "seq", None),
        P("grp"),
    )
    out_specs = (P("seq", "grp"), P(None, "grp", "seq"), P(None, "grp", "seq"))
    return jax.shard_map(
        on_device, mesh=mesh, in_specs=in_specs, out_specs=out_specs, check_vma=False
    )
```

profile of v0, /device:TPU:25, one launch (start us, length us, event | category | flops | bytes accessed | tf_op | source)
XLA Modules:
  0.0 1183.7 jit_solution(3349213730437571100)
XLA Ops:
  7.2 2.9 copy.233
  11.2 3.1 collective-permute-start.2
  14.4 3.9 copy.237
  22.4 6.4 copy.230
  28.8 2.9 slice.312
  31.7 2.8 copy.231
  41.1 6.8 all-to-all-start.1
  47.9 6.6 convert_element_type.41
  54.5 2.6 convert_element_type.42
  57.1 2.6 convert_element_type.43
  59.7 3.5 broadcast_select_fusion
  63.2 2.5 broadcast_select_fusion.1
  65.7 2.6 broadcast_select_fusion.2
  73.4 2.4 reduce-window.16
  79.9 2.1 fusion.73
  84.9 1.9 fusion.48
  92.8 2.5 divide_multiply_fusion.2
  95.4 3.0 divide_multiply_fusion.1
  100.3 2.8 copy.232
  103.2 23.0 %divide_multiply_fusion = f32[512,4096]{0,1:T(8,128)S(1)} fusion(f32[512,4096]{0,1:T(8,128)} %convert_element_type.41, f32[3,4096]{0,1:T(8,128)} %copy.232, f32[4096]{0:T(1024)S(1)} %bitcast.312, f32[4096]{0:T(1024)S(1)} %bitcast.310, f32[4096]{0:T(1024)S(1)} %bitcast.311, f32[4096]{0:T(1024)S(1)} %bitcast.309), kind=kLoop, calls=%fused_computation.63 | loop fusion | flops 29360128 | bytes 16891904 | tf_op jit(solution)/shard_map/jit(silu)/mul | solution.py:39
  126.2 3.2 copy-done.3
  129.4 4.5 multiply_bitcast_fusion
  133.9 10.6 reshape.522
  144.5 98.1 %while.26 = (s32[]{:T(128)}, f32[2,32,64,256]{3,2,1,0:T(8,128)}, f32[2,2,256,32,64]{2,4,3,1,0:T(8,128)}, f32[2,2,32,256]{3,0,2,1:T(2,128)S(1)}, f32[2,2,256,32,6...) while((s32[]{:T(128)}, f32[2,32,64,256]{3,2,1,0:T(8,128)}, ...), condition=%wide.region_3.4_spmd.clone, body=%wide.region_0.3_spmd.clone.sunk | while | flops 10092642304 | bytes 62923420 | solution.py:84
  147.3 9.8 constant_dynamic-slice_fusion.14
  157.1 21.4 %fusion.138 = f32[2,32,64,256]{3,2,1,0:T(8,128)} fusion(f32[2,256,256]{2,1,0:T(8,128)S(1)} %fusion.137, f32[2,32,256]{2,1,0:T(8,128)S(1)} %copy_bitcast_fusion.10, pred[256,256]{1,0:T(8,128)(4,1)S(1)} %iota_compare_fusion.4, f32[1,2,256,32,64]{2,0,4,3,1:T(1,128)} %constant_dynamic-slice_fusion.14), kind=kOutput, calls=%fused_computation.1.clone.1 | convolution fusion | flops 3238002688 | bytes 9043968 | tf_op jit(solution)/shard_map/vmap()/while/body/eval_jaxpr/kts,skp->tkp/dot_general | solution.py:65
  178.7 8.9 bitcast_dynamic-update-slice_fusion.2
  187.6 5.0 multiply_add_fusion.8
  194.9 9.9 constant_dynamic-slice_fusion.14
  204.8 21.3 %fusion.138 = f32[2,32,64,256]{3,2,1,0:T(8,128)} fusion(f32[2,256,256]{2,1,0:T(8,128)S(1)} %fusion.137, f32[2,32,256]{2,1,0:T(8,128)S(1)} %copy_bitcast_fusion.10, pred[256,256]{1,0:T(8,128)(4,1)S(1)} %iota_compare_fusion.4, f32[1,2,256,32,64]{2,0,4,3,1:T(1,128)} %constant_dynamic-slice_fusion.14), kind=kOutput, calls=%fused_computation.1.clone.1 | convolution fusion | flops 3238002688 | bytes 9043968 | tf_op jit(solution)/shard_map/vmap()/while/body/eval_jaxpr/kts,skp->tkp/dot_general | solution.py:65
  226.4 9.6 bitcast_dynamic-update-slice_fusion.2
  236.0 6.6 multiply_add_fusion.8
  242.7 2.6 broadcast_in_dim.135
  245.2 678.3 %while.25 = (s32[]{:T(128)}, f32[64,64,256]{2,1,0:T(8,128)}, f32[64,1,1]{0,2,1:T(1,128)S(1)}, f32[64,64,256]{2,1,0:T(8,128)}, s32[]{:T(128)}) while((s32[]{:T(128)}, f32[64,64,256]{2,1,0:T(8,128)}, f32[64,1,1]{0,2,1:T(1,128)S(1)}, f32[64,64,256]{2,1,0:T(8,128)}, s32[]{:T(128)}) %tuple.120), condition=%wide.region_7.8_spmd, body=%wide.region_6.7_spmd.sunk | while | flops 2097154 | bytes 29360484 | solution.py:182
  245.2 5.9 multiply_add_fusion.7
  251.1 3.0 collective-permute-start
  254.2 90.7 %collective-permute-done = f32[64,64,256]{2,1,0:T(8,128)} collective-permute-done((f32[64,64,256]{2,1,0:T(8,128)}, f32[64,64,256]{2,1,0:T(8,128)}, u32[]{:S(2)}, u32[]{:S(2)}) %collective-permute-start) | collective-permute-done | bytes 4194336 | tf_op jit(solution)/shard_map/while/body/eval_jaxpr/ppermute | solution.py:25
  344.9 5.9 multiply_add_fusion.7
  350.8 2.0 collective-permute-start
  352.8 90.8 %collective-permute-done = f32[64,64,256]{2,1,0:T(8,128)} collective-permute-done((f32[64,64,256]{2,1,0:T(8,128)}, f32[64,64,256]{2,1,0:T(8,128)}, u32[]{:S(2)}, u32[]{:S(2)}) %collective-permute-start) | collective-permute-done | bytes 4194336 | tf_op jit(solution)/shard_map/while/body/eval_jaxpr/ppermute | solution.py:25
  443.6 5.9 multiply_add_fusion.7
  451.4 90.0 %collective-permute-done = f32[64,64,256]{2,1,0:T(8,128)} collective-permute-done((f32[64,64,256]{2,1,0:T(8,128)}, f32[64,64,256]{2,1,0:T(8,128)}, u32[]{:S(2)}, u32[]{:S(2)}) %collective-permute-start) | collective-permute-done | bytes 4194336 | tf_op jit(solution)/shard_map/while/body/eval_jaxpr/ppermute | solution.py:25
  541.5 5.9 multiply_add_fusion.7
  549.2 89.1 %collective-permute-done = f32[64,64,256]{2,1,0:T(8,128)} collective-permute-done((f32[64,64,256]{2,1,0:T(8,128)}, f32[64,64,256]{2,1,0:T(8,128)}, u32[]{:S(2)}, u32[]{:S(2)}) %collective-permute-start) | collective-permute-done | bytes 4194336 | tf_op jit(solution)/shard_map/while/body/eval_jaxpr/ppermute | solution.py:25
  638.3 5.9 multiply_add_fusion.7
  646.1 88.2 %collective-permute-done = f32[64,64,256]{2,1,0:T(8,128)} collective-permute-done((f32[64,64,256]{2,1,0:T(8,128)}, f32[64,64,256]{2,1,0:T(8,128)}, u32[]{:S(2)}, u32[]{:S(2)}) %collective-permute-start) | collective-permute-done | bytes 4194336 | tf_op jit(solution)/shard_map/while/body/eval_jaxpr/ppermute | solution.py:25
  734.3 5.9 multiply_add_fusion.7
  742.1 87.3 %collective-permute-done = f32[64,64,256]{2,1,0:T(8,128)} collective-permute-done((f32[64,64,256]{2,1,0:T(8,128)}, f32[64,64,256]{2,1,0:T(8,128)}, u32[]{:S(2)}, u32[]{:S(2)}) %collective-permute-start) | collective-permute-done | bytes 4194336 | tf_op jit(solution)/shard_map/while/body/eval_jaxpr/ppermute | solution.py:25
  829.4 5.9 multiply_add_fusion.7
  837.2 86.3 %collective-permute-done = f32[64,64,256]{2,1,0:T(8,128)} collective-permute-done((f32[64,64,256]{2,1,0:T(8,128)}, f32[64,64,256]{2,1,0:T(8,128)}, u32[]{:S(2)}, u32[]{:S(2)}) %collective-permute-start) | collective-permute-done | bytes 4194336 | tf_op jit(solution)/shard_map/while/body/eval_jaxpr/ppermute | solution.py:25
  923.5 5.9 add_select_fusion
  934.5 4.5 all-to-all-start.2
  954.9 5.4 all-to-all-start
  963.5 2.0 fusion.95
  965.5 7.9 copy.327
  973.4 10.8 multiply_add_fusion.2
  984.3 3.1 fusion.44
  987.5 6.4 copy.280
  996.7 104.7 %all-reduce.5.cloned.1.call-done = f32[64,64,256]{2,1,0:T(8,128)} async-done(((f32[64,64,256]{2,1,0:T(8,128)}), f32[64,64,256]{2,1,0:T(8,128)}) %all-reduce.5.cloned.1.call-update) | async-done | bytes 4194320 | tf_op jit(solution)/shard_map/psum | solution.py:30
  1101.4 3.2 dynamic-slice_select_fusion
  1105.9 39.1 %psum.43 = f32[3,2048]{0,1:T(8,128)S(1)} all-reduce(f32[3,2048]{0,1:T(8,128)S(1)} %dynamic-slice_select_fusion.1), channel_id=1, replica_groups=mesh['seq'=8,'grp'=4] {'grp'}, use_global_device_ids=true, to_apply=%region_9.10 | all-reduce | flops 6144 | bytes 49152 | tf_op jit(solution)/shard_map/psum | solution.py:30
  1145.2 2.9 fusion.65
  1150.3 21.9 %all-reduce.7.cloned.1.call-done = f32[32,64,256]{2,1,0:T(8,128)} async-done(((f32[32,64,256]{2,1,0:T(8,128)}), f32[32,64,256]{2,1,0:T(8,128)}) %all-reduce.7.cloned.1.call-update) | async-done | bytes 2097168 | tf_op jit(solution)/shard_map/psum | solution.py:30
  1172.2 3.4 convolution_bitcast_fusion.1
  (257 shorter events, 77.5 us)
Async XLA Ops:
  7.2 31.6 %copy-start = (bf16[2,8,8192]{2,1,0:T(8,128)(2,1)S(1)}, bf16[2,8,8192]{2,1,0:T(8,128)(2,1)}, u32[]{:S(2)}) copy-start(bf16[2,8,8192]{2,1,0:T(8,128)(2,1)} %param.30) | copy-start | bytes 786436
  11.2 79.9 %collective-permute-start.2 = (f32[3,2048]{1,0:T(4,128)}, f32[3,2048]{1,0:T(4,128)}, u32[]{:S(2)}, u32[]{:S(2)}) collective-permute-start(f32[3,2048]{1,0:T(4,128)} %copy.234), channel_id=1, source_target_pairs={{0,4},{4,8},{8,12},{12,16},{16,20},{20,24},{24,28},{1,5},{5,9},{9,... | collective-permute-start | bytes 73736 | tf_op jit(solution)/shard_map/ppermute | solution.py:25
  20.5 70.6 %collective-permute-start.3 = (f32[3,2048]{1,0:T(4,128)}, f32[3,2048]{1,0:T(4,128)}, u32[]{:S(2)}, u32[]{:S(2)}) collective-permute-start(f32[3,2048]{1,0:T(4,128)} %copy.238), channel_id=1, source_target_pairs={{0,4},{4,8},{8,12},{12,16},{16,20},{20,24},{24,28},{1,5},{5,9},{9,... | collective-permute-start | bytes 73736 | tf_op jit(solution)/shard_map/ppermute | solution.py:25
  34.6 65.8 %collective-permute-start.1 = (f32[3,4096]{1,0:T(4,128)}, f32[3,4096]{1,0:T(4,128)}, u32[]{:S(2)}, u32[]{:S(2)}) collective-permute-start(f32[3,4096]{1,0:T(4,128)} %copy.231), channel_id=1, source_target_pairs={{0,4},{4,8},{8,12},{12,16},{16,20},{20,24},{24,28},{1,5},{5,9},{9,... | collective-permute-start | bytes 147464 | tf_op jit(solution)/shard_map/ppermute | solution.py:25
  40.3 14.2 %copy-start.14 = (f32[2,8,8,8]{3,0,2,1:T(2,128)}, f32[2,8,8,8]{3,0,2,1:T(2,128)S(1)}, u32[]{:S(2)}) copy-start(f32[2,8,8,8]{3,0,2,1:T(2,128)S(1)} %get-tuple-element.251) | copy-start | bytes 12292
  41.1 893.4 %all-to-all-start.1 = ((f32[8,1,128]{2,1,0:T(1,128)}), f32[8,1,128]{2,1,0:T(1,128)}, u32[]{:S(2)}, u32[]{:S(2)}) async-start(f32[8,1,128]{2,1,0:T(1,128)} %reshape.579), calls=%async_computation.1 | async-start | bytes 8192 | tf_op jit(solution)/shard_map/all_to_all | solution.py:263
  47.9 946.0 %all-reduce.9.cloned.1.call-start = ((), (), s32[]{:S(2)}) async-start(), calls=%async_computation.5 | async-start | bytes 8388608 | tf_op jit(solution)/shard_map/psum | solution.py:30
  54.5 2.6 copy-start.4
  68.3 2.9 copy-start.47
  68.3 3.0 copy-start.5
  68.3 1033.1 %all-reduce.5.cloned.1.call-start = ((), (), s32[]{:S(2)}) async-start(), calls=%async_computation.3 | async-start | bytes 8388608 | tf_op jit(solution)/shard_map/psum | solution.py:30
  72.8 12.1 %copy-start.43 = (pred[2,2]{1,0:T(4,128)(4,1)}, pred[2,2]{1,0:T(4,128)(4,1)S(1)}, u32[]{:S(2)}) copy-start(pred[2,2]{1,0:T(4,128)(4,1)S(1)} %iota_compare_fusion.2) | copy-start | bytes 16
  76.8 5.6 copy-start.15
  79.1 3.3 copy-start.7
  82.3 8.7 copy-start.10
  98.4 4.7 copy-start.20
  98.4 4.7 copy-start.21
  98.4 4.7 copy-start.22
  103.2 26.2 %copy-start.6 = (f32[64,512]{1,0:T(8,128)S(1)}, f32[64,512]{1,0:T(8,128)}, u32[]{:S(2)}) copy-start(f32[64,512]{1,0:T(8,128)} %param.22) | copy-start | bytes 393220
  126.2 3.2 copy-start.3
  178.7 8.9 copy-start.2
  226.4 9.6 copy-start.2
  242.7 2.6 copy-start.36
  251.1 93.8 %collective-permute-start = (f32[64,64,256]{2,1,0:T(8,128)}, f32[64,64,256]{2,1,0:T(8,128)}, u32[]{:S(2)}, u32[]{:S(2)}) collective-permute-start(f32[64,64,256]{2,1,0:T(8,128)} %multiply_add_fusion.7), channel_id=1, source_target_pairs={{0,4},{4,8},{8,12},{12,16},{16,20},{20,24},{24,28},{1,5},{5,9},{9,... | collective-permute-start | bytes 12582920 | tf_op jit(solution)/shard_map/while/body/eval_jaxpr/ppermute | solution.py:25
  350.8 92.9 %collective-permute-start = (f32[64,64,256]{2,1,0:T(8,128)}, f32[64,64,256]{2,1,0:T(8,128)}, u32[]{:S(2)}, u32[]{:S(2)}) collective-permute-start(f32[64,64,256]{2,1,0:T(8,128)} %multiply_add_fusion.7), channel_id=1, source_target_pairs={{0,4},{4,8},{8,12},{12,16},{16,20},{20,24},{24,28},{1,5},{5,9},{9,... | collective-permute-start | bytes 12582920 | tf_op jit(solution)/shard_map/while/body/eval_jaxpr/ppermute | solution.py:25
  449.5 91.9 %collective-permute-start = (f32[64,64,256]{2,1,0:T(8,128)}, f32[64,64,256]{2,1,0:T(8,128)}, u32[]{:S(2)}, u32[]{:S(2)}) collective-permute-start(f32[64,64,256]{2,1,0:T(8,128)} %multiply_add_fusion.7), channel_id=1, source_target_pairs={{0,4},{4,8},{8,12},{12,16},{16,20},{20,24},{24,28},{1,5},{5,9},{9,... | collective-permute-start | bytes 12582920 | tf_op jit(solution)/shard_map/while/body/eval_jaxpr/ppermute | solution.py:25
  547.3 91.0 %collective-permute-start = (f32[64,64,256]{2,1,0:T(8,128)}, f32[64,64,256]{2,1,0:T(8,128)}, u32[]{:S(2)}, u32[]{:S(2)}) collective-permute-start(f32[64,64,256]{2,1,0:T(8,128)} %multiply_add_fusion.7), channel_id=1, source_target_pairs={{0,4},{4,8},{8,12},{12,16},{16,20},{20,24},{24,28},{1,5},{5,9},{9,... | collective-permute-start | bytes 12582920 | tf_op jit(solution)/shard_map/while/body/eval_jaxpr/ppermute | solution.py:25
  644.2 90.1 %collective-permute-start = (f32[64,64,256]{2,1,0:T(8,128)}, f32[64,64,256]{2,1,0:T(8,128)}, u32[]{:S(2)}, u32[]{:S(2)}) collective-permute-start(f32[64,64,256]{2,1,0:T(8,128)} %multiply_add_fusion.7), channel_id=1, source_target_pairs={{0,4},{4,8},{8,12},{12,16},{16,20},{20,24},{24,28},{1,5},{5,9},{9,... | collective-permute-start | bytes 12582920 | tf_op jit(solution)/shard_map/while/body/eval_jaxpr/ppermute | solution.py:25
  740.2 89.2 %collective-permute-start = (f32[64,64,256]{2,1,0:T(8,128)}, f32[64,64,256]{2,1,0:T(8,128)}, u32[]{:S(2)}, u32[]{:S(2)}) collective-permute-start(f32[64,64,256]{2,1,0:T(8,128)} %multiply_add_fusion.7), channel_id=1, source_target_pairs={{0,4},{4,8},{8,12},{12,16},{16,20},{20,24},{24,28},{1,5},{5,9},{9,... | collective-permute-start | bytes 12582920 | tf_op jit(solution)/shard_map/while/body/eval_jaxpr/ppermute | solution.py:25
  835.2 88.3 %collective-permute-start = (f32[64,64,256]{2,1,0:T(8,128)}, f32[64,64,256]{2,1,0:T(8,128)}, u32[]{:S(2)}, u32[]{:S(2)}) collective-permute-start(f32[64,64,256]{2,1,0:T(8,128)} %multiply_add_fusion.7), channel_id=1, source_target_pairs={{0,4},{4,8},{8,12},{12,16},{16,20},{20,24},{24,28},{1,5},{5,9},{9,... | collective-permute-start | bytes 12582920 | tf_op jit(solution)/shard_map/while/body/eval_jaxpr/ppermute | solution.py:25
  929.4 4.2 copy-start.13
  929.4 11.1 copy-start.48
  929.4 18.5 %copy-start.18 = (f32[1,8,2048]{2,1,0:T(8,128)S(1)}, f32[1,8,2048]{2,1,0:T(8,128)}, u32[]{:S(2)}) copy-start(f32[1,8,2048]{2,1,0:T(8,128)} %get-tuple-element.245) | copy-start | bytes 196612
  929.4 19.3 %copy-start.17 = (f32[1,8,2048]{2,1,0:T(8,128)S(1)}, f32[1,8,2048]{2,1,0:T(8,128)}, u32[]{:S(2)}) copy-start(f32[1,8,2048]{2,1,0:T(8,128)} %get-tuple-element.246) | copy-start | bytes 196612
  929.4 20.0 %copy-start.8 = (f32[64,4,128]{2,0,1:T(8,128)S(1)}, f32[64,4,128]{2,0,1:T(8,128)}, u32[]{:S(2)}) copy-start(f32[64,4,128]{2,0,1:T(8,128)} %get-tuple-element.242) | copy-start | bytes 393220
  929.4 20.9 %copy-start.19 = (f32[2,8,8,8,2]{3,4,0,2,1:T(2,128)S(1)}, f32[2,8,8,8,2]{3,4,0,2,1:T(2,128)}, u32[]{:S(2)}) copy-start(f32[2,8,8,8,2]{3,4,0,2,1:T(2,128)} %fusion.48) | copy-start | bytes 24580
  934.5 20.4 %all-to-all-start.2 = ((f32[8,1,128]{2,1,0:T(1,128)}), f32[8,1,128]{2,1,0:T(1,128)}, u32[]{:S(2)}, u32[]{:S(2)}) async-start(f32[8,1,128]{2,1,0:T(1,128)} %reshape.581), calls=%async_computation.2 | async-start | bytes 8192 | tf_op jit(solution)/shard_map/all_to_all | solution.py:264
  940.5 8.9 copy-start.37
  940.5 8.9 copy-start.39
  954.9 193.4 %all-to-all-start = ((f32[1,2,8,64,128]{4,2,1,0,3:T(8,128)}), f32[1,2,8,64,128]{4,2,1,0,3:T(8,128)}, u32[]{:S(2)}, u32[]{:S(2)}) async-start(f32[1,2,8,64,128]{4,2,1,0,3:T(8,128)} %copy.266), calls=%async_computation | async-start | bytes 1048576 | tf_op jit(solution)/shard_map/all_to_all | solution.py:265
  960.3 211.9 %all-reduce.7.cloned.1.call-start = ((), (), s32[]{:S(2)}) async-start(), calls=%async_computation.4 | async-start | bytes 4194304 | tf_op jit(solution)/shard_map/psum | solution.py:30
  965.5 18.7 %slice-start = ((s8[8388608]{0:T(1024)(128)(4,1)}), s8[4194304]{0:T(1024)(128)(4,1)S(1)}, s32[]{:S(2)}) async-start(s8[8388608]{0:T(1024)(128)(4,1)} %bitcast.286), calls=%async_computation.6 | async-start | bytes 8388608
  973.4 10.8 slice-start.1
  973.4 10.9 copy-start.29
  987.4 6.4 copy-start.9
  987.4 8.0 copy-start.23
  987.4 8.0 copy-start.24
  987.4 8.1 copy-start.38
  987.4 8.1 copy-start.40
  987.4 8.1 copy-start.41
  987.5 8.1 copy-start.42
  987.5 8.8 copy-start.31
  987.5 8.8 copy-start.35
  1105.9 42.4 %copy-start.16 = (f32[8,2,8,8]{3,0,2,1:T(8,128)S(1)}, f32[8,2,8,8]{3,0,2,1:T(8,128)}, u32[]{:S(2)}) copy-start(f32[8,2,8,8]{3,0,2,1:T(8,128)} %get-tuple-element.205) | copy-start | bytes 12292
  1105.9 71.1 %copy-start.1 = (bf16[2,8,8192]{2,1,0:T(8,128)(2,1)S(1)}, bf16[2,8,8192]{2,1,0:T(8,128)(2,1)}, u32[]{:S(2)}) copy-start(bf16[2,8,8192]{2,1,0:T(8,128)(2,1)} %param.30) | copy-start | bytes 786436
  1145.1 3.2 copy-start.32
  1145.1 3.2 copy-start.33
  1145.1 4.5 copy-start.28
  1145.1 30.6 %copy-start.11 = (f32[1,8,32,64]{3,2,1,0:T(8,128)S(1)}, f32[1,8,32,64]{3,2,1,0:T(8,128)}, u32[]{:S(2)}) copy-start(f32[1,8,32,64]{3,2,1,0:T(8,128)} %squeeze.26) | copy-start | bytes 196612
  1145.1 30.6 %copy-start.12 = (f32[1,8,32,64]{3,2,1,0:T(8,128)S(1)}, f32[1,8,32,64]{3,2,1,0:T(8,128)}, u32[]{:S(2)}) copy-start(f32[1,8,32,64]{3,2,1,0:T(8,128)} %squeeze.28) | copy-start | bytes 196612
  1145.1 30.6 %copy-start.25 = (f32[8,32]{0,1:T(8,128)S(1)}, f32[8,32]{0,1:T(8,128)}, u32[]{:S(2)}) copy-start(f32[8,32]{0,1:T(8,128)} %copy.254) | copy-start | bytes 3076
  1145.1 30.6 %copy-start.26 = (f32[32,64]{1,0:T(8,128)S(1)}, f32[32,64]{1,0:T(8,128)}, u32[]{:S(2)}) copy-start(f32[32,64]{1,0:T(8,128)} %mul.724) | copy-start | bytes 24580
  1145.1 30.6 %copy-start.27 = (f32[32,64]{1,0:T(8,128)S(1)}, f32[32,64]{1,0:T(8,128)}, u32[]{:S(2)}) copy-start(f32[32,64]{1,0:T(8,128)} %mul.764) | copy-start | bytes 24580
  1145.2 30.6 %copy-start.46 = (f32[32]{0:T(128)S(1)}, f32[32]{0:T(128)}, u32[]{:S(2)}) copy-start(f32[32]{0:T(128)} %dynamic_slice.87) | copy-start | bytes 388
  (4 other events, 7.3 us)
Sparse Core Ops, SparseCore 0:
  68.5 156.8 all-reduce.8
  929.6 171.7 all-reduce.4
  1104.7 67.4 all-reduce.6
where the time goes:
time: 1190 us; the launch traced here: 1180 us
  waiting for transfers between devices  749 us (63%)
  other arithmetic  131 us (11%)
  local copies, waits for them, and re-layouts  113 us (9%)
  matrix products  96.4 us (8%)
  blocking collectives  39.1 us (3%)
  starting transfers between devices  38.6 us (3%)
  between operations  14.9 us (1%)
    ppermute x10, waiting for transfers between devices, passed_along(): lax.ppermute(value, axis, [(source, source + steps) for source in range(f...  622 us
    psum x3, waiting for transfers between devices, from_root(): return lax.psum(kept, axis)  127 us
    dot_general x2, matrix products, span_pass(): jnp.einsum('kts,skp->tkp', weights * intersection[None], inputs, precisio...  42.7 us
    add x7, other arithmetic, relay(): leaving = jnp.exp(section_decay)[:, None, None] * arriving + local_state  41.1 us
    psum x1, blocking collectives, from_root(): return lax.psum(kept, axis)  39.1 us
    unnamed x123, local copies, waits for them, and re-layouts  32.4 us
    mul x3, other arithmetic, causal_conv(): return jax.nn.silu(accumulated)  28.6 us
  transfers between devices with their start and end apart: 16, of which 9 were waited for; matrix products, arithmetic and copies ran while one was open for 28% of the time, Pallas kernels for 0%

commit v1 on v0

--- a/solution.py
+++ b/solution.py
@@ -1,6 +1,10 @@
+import functools
+
 import jax
 import jax.numpy as jnp
 from jax import lax
+from jax.experimental import pallas as pl
+from jax.experimental.pallas import tpu as pltpu
 from jax.sharding import PartitionSpec as P
 
 HEADS = 256
@@ -15,7 +19,8 @@
 STEPS = 2
 
 
-HIGH = lax.Precision.HIGHEST
+HIGH = lax.Precision.HIGH
+MESH = pl.DeviceIdType.MESH
 NEG = -1e30
 
 
@@ -108,6 +113,206 @@
     per_group = HEADS // GROUPS
     group_count = max(1, head_count // per_group)
     return (head_begin // per_group, group_count, head_count // group_count)
+
+
+def relay_kernel(
+    count,
+    groups,
+    chunk,
+    factor_ref,
+    local_ref,
+    incoming_ref,
+    prefix_ref,
+    leaving,
+    send_sem,
+    recv_sem,
+    final_send,
+    prefix_recv,
+    fan_send,
+):
+    me = lax.axis_index("seq")
+    mine = lax.axis_index("grp")
+    local_heads = local_ref.shape[0]
+    state_heads = prefix_ref.shape[0]
+    shares = local_heads // state_heads
+    pieces = local_heads // chunk
+    own_pieces = state_heads // chunk
+    last = count - 1
+    is_last = me == last
+    is_root = me // shares == mine
+
+    barrier = pltpu.get_barrier_semaphore()
+
+    def greet(where):
+        pl.semaphore_signal(barrier, inc=1, device_id=where, device_id_type=MESH)
+
+    @pl.when(me > 0)
+    def _():
+        greet((me - 1, mine))
+
+    @pl.when(me < last)
+    def _():
+        greet((me + 1, mine))
+
+    for other in range(1, groups):
+        greet((me, lax.rem(mine + other, groups)))
+
+    @pl.when(jnp.logical_and(is_root, me < last))
+    def _():
+        greet((last, mine))
+
+    for share in range(shares):
+        owner = mine * shares + share
+
+        @pl.when(jnp.logical_and(is_last, owner != last))
+        def _():
+            greet((owner, mine))
+
+    expected = (
+        (me > 0).astype(jnp.int32)
+        + (me < last).astype(jnp.int32)
+        + (groups - 1)
+        + jnp.logical_and(is_root, me < last).astype(jnp.int32)
+    )
+    for share in range(shares):
+        expected = expected + jnp.logical_and(is_last, mine * shares + share != last).astype(
+            jnp.int32
+        )
+    pl.semaphore_wait(barrier, expected)
+
+    def pass_on(piece, target):
+        rows = pl.ds(piece * chunk, chunk)
+        return pltpu.make_async_remote_copy(
+            src_ref=leaving.at[rows],
+            dst_ref=incoming_ref.at[rows],
+            send_sem=send_sem.at[piece],
+            recv_sem=recv_sem.at[piece],
+            device_id=(target, mine),
+            device_id_type=MESH,
+        )
+
+    def final_copy(piece, own_piece, owner):
+        return pltpu.make_async_remote_copy(
+            src_ref=leaving.at[pl.ds(piece * chunk, chunk)],
+            dst_ref=prefix_ref.at[pl.ds(own_piece * chunk, chunk)],
+            send_sem=final_send.at[piece],
+            recv_sem=prefix_recv.at[own_piece],
+            device_id=(owner, mine),
+            device_id_type=MESH,
+        )
+
+    def fan_copy(own_piece, other):
+        rows = pl.ds(own_piece * chunk, chunk)
+        return pltpu.make_async_remote_copy(
+            src_ref=prefix_ref.at[rows],
+            dst_ref=prefix_ref.at[rows],
+            send_sem=fan_send.at[other - 1, own_piece],
+            recv_sem=prefix_recv.at[own_piece],
+            device_id=(me, lax.rem(mine + other, groups)),
+            device_id_type=MESH,
+        )
+
+    def one_piece(piece, carry):
+        rows = pl.ds(piece * chunk, chunk)
+
+        @pl.when(me == 0)
+        def _():
+            incoming_ref[rows] = jnp.zeros((chunk,) + local_ref.shape[1:], jnp.float32)
+
+        @pl.when(me > 0)
+        def _():
+            pass_on(piece, me).wait_recv()
+
+        for head in range(chunk):
+            at = piece * chunk + head
+            leaving[at] = factor_ref[at] * incoming_ref[at] + local_ref[at]
+
+        @pl.when(me < last)
+        def _():
+            pass_on(piece, me + 1).start()
+
+        owner = mine * shares + piece // own_pieces
+        own_piece = lax.rem(piece, own_pieces)
+
+        @pl.when(jnp.logical_and(is_last, owner != last))
+        def _():
+            final_copy(piece, own_piece, owner).start()
+
+        @pl.when(jnp.logical_and(is_last, owner == last))
+        def _():
+            prefix_ref[pl.ds(own_piece * chunk, chunk)] = leaving[rows]
+            for other in range(1, groups):
+                fan_copy(own_piece, other).start()
+
+        return carry
+
+    lax.fori_loop(0, pieces, one_piece, 0)
+
+    def one_arrival(own_piece, carry):
+        @pl.when(jnp.logical_not(jnp.logical_and(is_root, is_last)))
+        def _():
+            final_copy(own_piece, own_piece, me).wait_recv()
+
+        @pl.when(jnp.logical_and(is_root, me < last))
+        def _():
+            for other in range(1, groups):
+                fan_copy(own_piece, other).start()
+
+        return carry
+
+    lax.fori_loop(0, own_pieces, one_arrival, 0)
+
+    def drain(piece, carry):
+        owner = mine * shares + piece // own_pieces
+
+        @pl.when(me < last)
+        def _():
+            pass_on(piece, me).wait_send()
+
+        @pl.when(jnp.logical_and(is_last, owner != last))
+        def _():
+            final_copy(piece, lax.rem(piece, own_pieces), owner).wait_send()
+
+        return carry
+
+    lax.fori_loop(0, pieces, drain, 0)
+
+    @pl.when(is_root)
+    def _():
+        def drain_fan(own_piece, carry):
+            for other in range(1, groups):
+                fan_copy(own_piece, other).wait_send()
+            return carry
+
+        lax.fori_loop(0, own_pieces, drain_fan, 0)
+
+
+def relay_states(factor, local_state, state_heads, count, groups):
+    local_heads = local_state.shape[0]
+    chunk = 2
+    pieces = local_heads // chunk
+    own_pieces = state_heads // chunk
+    vmem = pl.BlockSpec(memory_space=pltpu.VMEM)
+    return pl.pallas_call(
+        functools.partial(relay_kernel, count, groups, chunk),
+        out_shape=(
+            jax.ShapeDtypeStruct(local_state.shape, jnp.float32),
+            jax.ShapeDtypeStruct((state_heads,) + local_state.shape[1:], jnp.float32),
+        ),
+        in_specs=[pl.BlockSpec(memory_space=pltpu.SMEM), vmem],
+        out_specs=(vmem, vmem),
+        scratch_shapes=[
+            pltpu.VMEM(local_state.shape, jnp.float32),
+            pltpu.SemaphoreType.DMA((pieces,)),
+            pltpu.SemaphoreType.DMA((pieces,)),
+            pltpu.SemaphoreType.DMA((pieces,)),
+            pltpu.SemaphoreType.DMA((own_pieces,)),
+            pltpu.SemaphoreType.DMA((groups - 1, own_pieces)),
+        ],
+        compiler_params=pltpu.CompilerParams(
+            collective_id=0, has_side_effects=True, vmem_limit_bytes=40 * 1024 * 1024
+        ),
+    )(factor, local_state)
 
 
 def on_device(
@@ -140,8 +345,25 @@
     source_x = pre_x.astype(jnp.float32)
     full_b = pre_b.astype(jnp.float32)
     full_c = pre_c.astype(jnp.float32)
-    tail_rows = (source_x[section - edge :], full_b[section - edge :], full_c[section - edge :])
-    leading = passed_along((tail_rows[0], tail_rows[1], tail_rows[2]), "seq", 1)
+    own_b = lax.dynamic_slice_in_dim(full_b, group_begin * STATE, group_count * STATE, 1)
+    own_c = lax.dynamic_slice_in_dim(full_c, group_begin * STATE, group_count * STATE, 1)
+    edge_rows = jnp.concatenate(
+        [source_x[section - edge :], own_b[section - edge :], own_c[section - edge :]], axis=1
+    )
+    edge_rows = passed_along(edge_rows, "seq", 1)
+    split_b = local_heads * HDIM
+    split_c = split_b + group_count * STATE
+    leading = (edge_rows[:, :split_b], edge_rows[:, split_b:split_c], edge_rows[:, split_c:])
+    is_end = seq_index == seq_count - 1
+    shown_x = jnp.where(is_end, source_x[section - edge :], 0.0)
+    shown_bc = jnp.where(
+        jnp.logical_and(is_end, grp_index == 0),
+        jnp.concatenate([full_b[section - edge :], full_c[section - edge :]], axis=1),
+        0.0,
+    )
+    tails = jnp.concatenate([jnp.zeros((edge, x_offset), jnp.float32), shown_bc], axis=1)
+    tails = lax.dynamic_update_slice_in_dim(tails, shown_x, head_begin * HDIM, 1)
+    tails = lax.psum(tails, ("seq", "grp"))
     kernel_x = lax.dynamic_slice_in_dim(conv_taps, head_begin * HDIM, local_heads * HDIM, 1)
     kernel_b = lax.dynamic_slice_in_dim(
         conv_taps, x_offset + group_begin * STATE, group_count * STATE, 1
@@ -150,16 +372,8 @@
         conv_taps, c_offset + group_begin * STATE, group_count * STATE, 1
     )
     conv_x = causal_conv(leading[0], source_x, kernel_x)
-    conv_b = causal_conv(
-        lax.dynamic_slice_in_dim(leading[1], group_begin * STATE, group_count * STATE, 1),
-        lax.dynamic_slice_in_dim(full_b, group_begin * STATE, group_count * STATE, 1),
-        kernel_b,
-    )
-    conv_c = causal_conv(
-        lax.dynamic_slice_in_dim(leading[2], group_begin * STATE, group_count * STATE, 1),
-        lax.dynamic_slice_in_dim(full_c, group_begin * STATE, group_count * STATE, 1),
-        kernel_c,
-    )
+    conv_b = causal_conv(leading[1], own_b, kernel_b)
+    conv_c = causal_conv(leading[2], own_c, kernel_c)
     rates = lax.dynamic_slice_in_dim(decay_rate, head_begin, local_heads, 0)
     gains = lax.dynamic_slice_in_dim(skip_gain, head_begin, local_heads, 0)
     log_decay = -pre_dt * rates[:, None]
@@ -175,11 +389,10 @@
     cumulative = jnp.cumsum(log_decay, axis=1)
     section_decay = cumulative[:, -1]
 
-    def relay(counter, arriving):
-        leaving = jnp.exp(section_decay)[:, None, None] * arriving + local_state
-        return passed_along(leaving, "seq", 1)
-
-    incoming = lax.fori_loop(0, seq_count - 1, relay, jnp.zeros_like(local_state))
+    state_heads = HEADS // seq_count
+    incoming, prefix_state = relay_states(
+        jnp.exp(section_decay), local_state, state_heads, seq_count, lax.axis_size("grp")
+    )
     incoming_groups = incoming.reshape(group_count, heads_each, HDIM, STATE)
     from_before = jnp.einsum("gsn,gkpn->gskp", readout, incoming_groups, precision=HIGH)
     decay_factor = jnp.exp(cumulative).reshape(group_count, heads_each, section).transpose(0, 2, 1)
@@ -189,22 +402,11 @@
         + gains[None, :, None] * head_inputs
     )
     pre_y = combined.reshape(section, local_heads * HDIM).astype(jnp.bfloat16)
-    closing = jnp.exp(section_decay)[:, None, None] * incoming + local_state
-    final_state, tail_x, tail_b, tail_c = (
-        from_root(closing, "seq", seq_count - 1),
-        from_root(tail_rows[0], "seq", seq_count - 1),
-        from_root(tail_rows[1], "seq", seq_count - 1),
-        from_root(tail_rows[2], "seq", seq_count - 1),
-    )
-    state_heads = HEADS // seq_count
-    root_group = seq_index * state_heads // local_heads
-    offset_heads = seq_index * state_heads - root_group * local_heads
-    own_state = lax.dynamic_slice_in_dim(final_state, offset_heads, state_heads, 0)
-    own_tail = lax.dynamic_slice_in_dim(tail_x, offset_heads * HDIM, state_heads * HDIM, 1)
-    prefix_state, prefix_tail = (
-        from_root(own_state, "grp", root_group),
-        from_root(own_tail, "grp", root_group),
-    )
+    prefix_tail = lax.dynamic_slice_in_dim(
+        tails, seq_index * state_heads * HDIM, state_heads * HDIM, 1
+    )
+    tail_b = tails[:, x_offset:c_offset]
+    tail_c = tails[:, c_offset:]
     rows_here = dec_x.shape[1]
     dec_begin = seq_index * state_heads
     dgroup_begin, dgroup_count, dheads_each = group_layout(dec_begin, state_heads)

time: 1190 us -> 489 us (0.41)
  waiting for transfers between devices: 749 us -> 0.99 us
  Pallas kernels: 0 us -> 195 us
  other arithmetic: 131 us -> 76 us
  matrix products: 96.4 us -> 51.1 us
  blocking collectives: 39.1 us -> 0 us
  starting transfers between devices: 38.6 us -> 20.8 us
    ppermute x10 -> x1, waiting for transfers between devices: 622 us -> 0.01 us  [passed_along(): lax.ppermute(value, axis, [(source, source + steps) for source in range(f...]
    pallas_call x0 -> x1, Pallas kernels: none -> 195 us  [relay_states(): pl.pallas_call(functools.partial(relay_kernel, count, groups, chunk), out...]
    psum x3 -> x1, waiting for transfers between devices: 127 us -> 0.01 us  [on_device(): tails = lax.psum(tails, ('seq', 'grp'))]
    add x7 -> x0, other arithmetic: 41.1 us -> none  [relay(): leaving = jnp.exp(section_decay)[:, None, None] * arriving + local_state]
    psum x1 -> x0, blocking collectives: 39.1 us -> none  [from_root(): return lax.psum(kept, axis)]
    dot_general x2, matrix products: 42.7 us -> 24.4 us  [span_pass(): jnp.einsum('kts,skp->tkp', weights * intersection[None], inputs, precisio...]
    ppermute x10 -> x1, starting transfers between devices: 21.6 us -> 3.61 us  [passed_along(): lax.ppermute(value, axis, [(source, source + steps) for source in range(f...]
    select_n x6 -> x1, other arithmetic: 18.9 us -> 1.41 us  [on_device(): jnp.where(jnp.logical_and(is_end, grp_index == 0), jnp.concatenate([full_...]
  transfers between devices with their start and end apart: 16 -> 5, of which waited for: 9 -> 1; matrix products, arithmetic and copies ran while one was open for 28% -> 49% of each run, Pallas kernels for 0% -> 40%
where the time goes in v1:
time: 489 us; the launch traced here: 483 us
  Pallas kernels  195 us (40%)
  local copies, waits for them, and re-layouts  123 us (25%)
  other arithmetic  76 us (16%)
  matrix products  51.1 us (10%)
  starting transfers between devices  20.8 us (4%)
  between operations  15.3 us (3%)
    pallas_call x1, Pallas kernels, relay_states(): pl.pallas_call(functools.partial(relay_kernel, count, groups, chunk), out...  195 us
    unnamed x141, local copies, waits for them, and re-layouts  35.9 us
    mul x3, other arithmetic, causal_conv(): return jax.nn.silu(accumulated)  27.5 us
    dot_general x2, matrix products, span_pass(): jnp.einsum('kts,skp->tkp', weights * intersection[None], inputs, precisio...  24.4 us
    dynamic_slice x4, local copies, waits for them, and re-layouts, run_spans(): ssm_state, results = lax.scan(span_pass, ssm_state, blocks)  19.9 us
    reshape x1, local copies, waits for them, and re-layouts, run_spans(): inputs.reshape(block_total, SPAN, heads_here, head_width)  10.6 us
  transfers between devices with their start and end apart: 5, of which 1 were waited for; matrix products, arithmetic and copies ran while one was open for 49% of the time, Pallas kernels for 40%

profile of v1, /device:TPU:25, one launch (start us, length us, event | category | flops | bytes accessed | tf_op | source)
XLA Modules:
  0.0 483.0 jit_solution(3155270246166135467)
XLA Ops:
  7.2 2.8 fusion.112
  10.4 1.5 fusion.116
  12.8 5.5 %all-to-all-start.1 = ((f32[8,1,128]{2,1,0:T(1,128)}), f32[8,1,128]{2,1,0:T(1,128)S(1)}, u32[]{:S(2)}, u32[]{:S(2)}) async-start(f32[8,1,128]{2,1,0:T(1,128)} %reshape.559), calls=%async_computation.1 | async-start | bytes 8192 | tf_op jit(solution)/shard_map/all_to_all | solution.py:465
  18.3 2.9 copy.285
  21.4 3.9 copy.286
  25.3 1.0 dynamic-slice.2
  26.5 6.4 %copy.284 = bf16[512,4096]{0,1:T(8,128)(2,1)} copy(bf16[512,4096]{1,0:T(8,128)(2,1)} %param.17) | data formatting | bytes 8388608 | tf_op args[0]
  32.9 2.9 slice.341
  35.8 2.2 copy.287
  38.7 3.6 collective-permute-start
  42.5 2.2 slice.360
  44.7 6.7 %convert_element_type.31 = f32[512,4096]{0,1:T(8,128)} convert(bf16[512,4096]{0,1:T(8,128)(2,1)} %copy.284) | non-fusion elementwise | flops 2097152 | bytes 12582912 | tf_op jit(solution)/shard_map/convert_element_type | solution.py:345
  51.4 1.4 maximum_select_fusion
  52.8 6.8 %concatenate.25 = f32[3,20480]{0,1:T(8,128)} pad(f32[3,4096]{0,1:T(8,128)S(1)} %maximum_select_fusion, f32[]{:T(128)} %constant.93.clone.1), padding=0_0x16384_0 | pad | bytes 294916 | tf_op jit(solution)/shard_map/concatenate | solution.py:364
  59.6 3.5 select_dynamic-update-slice_fusion
  64.8 4.2 convert_element_type.33
  69.0 3.1 convert_element_type.32
  74.4 1.2 reduce-window.16
  76.8 1.4 fusion.115
  79.9 1.8 constant_dynamic-slice_fusion.3
  81.8 1.6 constant_dynamic-slice_fusion.2
  83.9 2.2 fusion.110
  87.0 1.3 fusion.48
  88.2 1.8 constant_dynamic-slice_fusion.8
  90.0 1.3 dynamic-slice_convert_fusion
  91.4 1.5 fusion.113
  103.7 1.4 copy.372
  105.0 1.4 copy.371
  106.4 1.3 copy.370
  108.7 1.1 copy.321
  109.9 4.6 all-to-all-start.2
  116.1 1.0 all-to-all-done.2
  117.1 7.1 %all-to-all-start = ((f32[1,2,8,64,128]{4,2,1,0,3:T(8,128)}), f32[1,2,8,64,128]{4,2,1,0,3:T(8,128)}, u32[]{:S(2)}, u32[]{:S(2)}) async-start(f32[1,2,8,64,128]{4,2,1,0,3:T(8,128)} %copy.321), calls=%async_computation | async-start | bytes 1048576 | tf_op jit(solution)/shard_map/all_to_all | solution.py:467
  126.0 1.0 fusion.94
  129.3 2.6 divide_multiply_fusion.2
  132.2 2.1 divide_multiply_fusion.1
  135.6 2.0 copy.290
  137.6 22.9 %divide_multiply_fusion = f32[512,4096]{0,1:T(8,128)S(1)} fusion(f32[512,4096]{0,1:T(8,128)} %convert_element_type.31, f32[3,4096]{0,1:T(8,128)} %copy.290, f32[4096]{0:T(1024)S(1)} %bitcast.308, f32[4096]{0:T(1024)S(1)} %bitcast.306, f32[4096]{0:T(1024)S(1)} %bitcast.307, f32[4096]{0:T(1024)S(1)} %bitcast.305), kind=kLoop, calls=%fused_computation.62 | loop fusion | flops 29360128 | bytes 16891904 | tf_op jit(solution)/shard_map/jit(silu)/mul | solution.py:44
  160.5 3.3 copy-done.6
  163.7 4.6 multiply_bitcast_fusion
  168.3 10.6 %reshape.503 = f32[2,2,256,32,64]{2,1,4,3,0:T(2,128)} reshape(f32[2,512,32,64]{1,3,2,0:T(8,128)} %multiply_bitcast_fusion) | data formatting | bytes 16777216 | tf_op jit(solution)/shard_map/vmap()/reshape | solution.py:84
  179.0 67.0 %while.13 = (s32[]{:T(128)}, f32[2,32,64,256]{3,2,1,0:T(8,128)}, f32[2,2,256,32,64]{2,4,3,1,0:T(8,128)}, f32[2,2,32,256]{3,0,2,1:T(2,128)S(1)}, f32[2,2,256,32,6...) while((s32[]{:T(128)}, f32[2,32,64,256]{3,2,1,0:T(8,128)}, ...), condition=%wide.region_3.4_spmd.clone, body=%wide.region_0.3_spmd.clone.sunk | while | flops 5059477504 | bytes 96478432 | solution.py:89
  179.2 1.2 reduce-window.26
  181.5 9.8 %constant_dynamic-slice_fusion.12 = f32[1,2,256,32,64]{2,0,4,3,1:T(1,128)} fusion(f32[2,2,256,32,64]{2,0,4,3,1:T(2,128)} %get-tuple-element.286, s32[]{:T(128)S(6)} %copy.454), kind=kLoop, calls=%fused_computation.41.clone.1 | loop fusion | bytes 8388612 | tf_op jit(solution)/shard_map/vmap()/while/body/jit(dynamic_index_in_dim)/dynamic_slice | solution.py:89
  191.2 12.2 %fusion.140 = f32[2,32,64,256]{3,2,1,0:T(8,128)S(1)} fusion(f32[2,256,256]{2,1,0:T(8,128)S(1)} %fusion.139, f32[2,32,256]{2,1,0:T(8,128)S(1)} %copy_bitcast_fusion.10, pred[256,256]{1,0:T(8,128)(4,1)S(1)} %iota_compare_fusion.4, f32[1,2,256,32,64]{2,0,4,3,1:T(1,128)} %constant_dynamic-slice_fusion.12), kind=kOutput, calls=%fused_computation.clone.1 | convolution fusion | flops 1627389952 | bytes 9043968 | tf_op jit(solution)/shard_map/vmap()/while/body/eval_jaxpr/kts,skp->tkp/dot_general | solution.py:70
  203.5 4.1 bitcast_dynamic-update-slice_fusion.2
  207.6 2.6 multiply_add_fusion.5
  210.2 2.0 copy-done.3
  212.3 1.2 reduce-window.26
  214.5 10.0 %constant_dynamic-slice_fusion.12 = f32[1,2,256,32,64]{2,0,4,3,1:T(1,128)} fusion(f32[2,2,256,32,64]{2,0,4,3,1:T(2,128)} %get-tuple-element.286, s32[]{:T(128)S(6)} %copy.454), kind=kLoop, calls=%fused_computation.41.clone.1 | loop fusion | bytes 8388612 | tf_op jit(solution)/shard_map/vmap()/while/body/jit(dynamic_index_in_dim)/dynamic_slice | solution.py:89
  224.6 12.2 %fusion.140 = f32[2,32,64,256]{3,2,1,0:T(8,128)S(1)} fusion(f32[2,256,256]{2,1,0:T(8,128)S(1)} %fusion.139, f32[2,32,256]{2,1,0:T(8,128)S(1)} %copy_bitcast_fusion.10, pred[256,256]{1,0:T(8,128)(4,1)S(1)} %iota_compare_fusion.4, f32[1,2,256,32,64]{2,0,4,3,1:T(1,128)} %constant_dynamic-slice_fusion.12), kind=kOutput, calls=%fused_computation.clone.1 | convolution fusion | flops 1627389952 | bytes 9043968 | tf_op jit(solution)/shard_map/vmap()/while/body/eval_jaxpr/kts,skp->tkp/dot_general | solution.py:70
  236.8 4.3 bitcast_dynamic-update-slice_fusion.2
  241.1 2.6 multiply_add_fusion.5
  243.7 2.0 copy-done.3
  246.0 4.7 copy.382
  250.7 195.0 %shard_map.166 = (f32[64,64,256]{2,1,0:T(8,128)S(1)}, f32[32,64,256]{2,1,0:T(8,128)S(1)}) custom-call(f32[64]{0:T(128)S(1)} %fusion.98.factor_ref, f32[64,64,256]{2,1,0:T(8,128)S(1)} %bitcast.279), custom_call_target="tpu_custom_call" | custom-call | tf_op jit(solution)/shard_map/pallas_call | solution.py:296
  445.7 6.0 %multiply_add_fusion.1 = f32[2,512,32,64]{1,3,2,0:T(8,128)} fusion(f32[2,512,32,64]{1,3,2,0:T(8,128)S(1)} %bitcast.284, f32[2,512,32]{1,2,0:T(8,128)S(1)} %bitcast.298, f32[2,512,256,1]{1,2,3,0:T(8,128)S(1)} %bitcast.288, f32[2,32,64,256]{3,2,1,0:T(8,128)S(1)} %bitcast.278), kind=kOutput, calls=%fused_computation.60 | convolution fusion | flops 3225419776 | bytes 22151168 | tf_op jit(solution)/shard_map/gsn,gkpn->gskp/dot_general | solution.py:397
  451.8 5.3 %fusion.44 = bf16[512,4096]{0,1:T(8,128)(2,1)} fusion(f32[2,512,32,64]{1,3,2,0:T(8,128)} %multiply_add_fusion.1, f32[512,4096]{0,1:T(8,128)S(1)} %bitcast.283, f32[4096]{0:T(1024)S(1)} %copy-done.36), kind=kLoop, calls=%fused_computation.59 | loop fusion | flops 6291456 | bytes 20987904 | tf_op jit(solution)/shard_map/convert_element_type | solution.py:404
  457.0 6.4 %copy.335 = bf16[512,4096]{1,0:T(8,128)(2,1)} copy(bf16[512,4096]{0,1:T(8,128)(2,1)} %fusion.44) | data formatting | bytes 8388608
  463.4 3.9 fusion.65
  467.6 1.8 fusion.111
  469.4 1.6 fusion.88
  471.7 0.9 convolution_bitcast_fusion.1
  473.9 1.3 fusion.70
  (253 shorter events, 34.6 us)
Async XLA Ops:
  7.2 3.2 copy-start
  12.0 6.3 %copy-start.21 = (f32[2,8,8,8]{3,0,2,1:T(2,128)}, f32[2,8,8,8]{3,0,2,1:T(2,128)S(1)}, u32[]{:S(2)}) copy-start(f32[2,8,8,8]{3,0,2,1:T(2,128)S(1)} %get-tuple-element.207) | copy-start | bytes 12292
  12.8 97.1 %all-to-all-start.1 = ((f32[8,1,128]{2,1,0:T(1,128)}), f32[8,1,128]{2,1,0:T(1,128)S(1)}, u32[]{:S(2)}, u32[]{:S(2)}) async-start(f32[8,1,128]{2,1,0:T(1,128)} %reshape.559), calls=%async_computation.1 | async-start | bytes 8192 | tf_op jit(solution)/shard_map/all_to_all | solution.py:465
  18.3 445.1 %all-reduce.3.cloned.1.call-start = ((), (), s32[]{:S(2)}) async-start(), calls=%async_computation.3 | async-start | bytes 20971520 | tf_op jit(solution)/shard_map/psum | solution.py:366
  38.7 88.9 %collective-permute-start = (f32[3,5120]{1,0:T(4,128)}, f32[3,5120]{1,0:T(4,128)}, u32[]{:S(2)}, u32[]{:S(2)}) collective-permute-start(f32[3,5120]{1,0:T(4,128)} %pad_maximum_fusion.3), channel_id=1, source_target_pairs={{0,4},{4,8},{8,12},{12,16},{16,20},{20,24},{24,28},{1,5},{5,9},{9,... | collective-permute-start | bytes 184328 | tf_op jit(solution)/shard_map/ppermute | solution.py:30
  69.0 4.0 copy-start.43
  69.0 9.2 %copy-start.10 = (bf16[1,8,64,1024]{3,2,1,0:T(8,128)(2,1)S(1)}, bf16[1,8,64,1024]{3,2,1,0:T(8,128)(2,1)}, u32[]{:S(2)}) copy-start(bf16[1,8,64,1024]{3,2,1,0:T(8,128)(2,1)} %get-tuple-element.168) | copy-start | bytes 3145732
  72.2 6.4 %copy-start.14 = (f32[2,8,8,8,64]{4,3,0,2,1:T(8,128)S(1)}, f32[2,8,8,8,64]{4,3,0,2,1:T(8,128)}, u32[]{:S(2)}) copy-start(f32[2,8,8,8,64]{4,3,0,2,1:T(8,128)} %get-tuple-element.208) | copy-start | bytes 786436
  72.2 6.4 %copy-start.22 = (f32[2,8,8,8]{3,0,2,1:T(2,128)S(1)}, f32[2,8,8,8]{3,0,2,1:T(2,128)}, u32[]{:S(2)}) copy-start(f32[2,8,8,8]{3,0,2,1:T(2,128)} %copy-done.21) | copy-start | bytes 12292
  72.2 6.5 %copy-start.54 = (pred[8,64]{1,0:T(8,128)(4,1)S(1)}, pred[8,64]{1,0:T(8,128)(4,1)}, u32[]{:S(2)}) copy-start(pred[8,64]{1,0:T(8,128)(4,1)} %copy-done.53) | copy-start | bytes 1540
  78.2 8.7 %copy-start.55 = (pred[2,2]{1,0:T(4,128)(4,1)S(1)}, pred[2,2]{1,0:T(4,128)(4,1)}, u32[]{:S(2)}) copy-start(pred[2,2]{1,0:T(4,128)(4,1)} %iota_compare_fusion.2) | copy-start | bytes 16
  79.1 13.8 %copy-start.60 = (f32[256]{0:T(256)S(1)}, f32[256]{0:T(256)}, u32[]{:S(2)}) copy-start(f32[256]{0:T(256)} %param.22) | copy-start | bytes 3076
  79.8 21.4 %copy-start.17 = (f32[64,512]{1,0:T(8,128)S(1)}, f32[64,512]{1,0:T(8,128)}, u32[]{:S(2)}) copy-start(f32[64,512]{1,0:T(8,128)} %negate_multiply_fusion) | copy-start | bytes 393220
  79.9 21.5 %copy-start.16 = (f32[64,4,128]{2,0,1:T(8,128)S(1)}, f32[64,4,128]{2,0,1:T(8,128)}, u32[]{:S(2)}) copy-start(f32[64,4,128]{2,0,1:T(8,128)} %get-tuple-element.196) | copy-start | bytes 393220
  79.9 22.3 %copy-start.24 = (f32[1,8,2048]{2,1,0:T(8,128)S(1)}, f32[1,8,2048]{2,1,0:T(8,128)}, u32[]{:S(2)}) copy-start(f32[1,8,2048]{2,1,0:T(8,128)} %get-tuple-element.201) | copy-start | bytes 196612
  79.9 23.1 %copy-start.23 = (f32[1,8,2048]{2,1,0:T(8,128)S(1)}, f32[1,8,2048]{2,1,0:T(8,128)}, u32[]{:S(2)}) copy-start(f32[1,8,2048]{2,1,0:T(8,128)} %get-tuple-element.202) | copy-start | bytes 196612
  88.2 15.5 %copy-start.40 = (f32[1,2048]{1,0:T(1,128)S(1)}, f32[1,2048]{1,0:T(1,128)}, u32[]{:S(2)}) copy-start(f32[1,2048]{1,0:T(1,128)} %get-tuple-element.161) | copy-start | bytes 24580
  88.2 16.8 %copy-start.39 = (f32[1,2048]{1,0:T(1,128)S(1)}, f32[1,2048]{1,0:T(1,128)}, u32[]{:S(2)}) copy-start(f32[1,2048]{1,0:T(1,128)} %get-tuple-element.173) | copy-start | bytes 24580
  92.9 7.6 %copy-start.45 = (f32[1,256]{1,0:T(1,128)}, f32[1,256]{1,0:T(1,128)S(1)}, u32[]{:S(2)}) copy-start(f32[1,256]{1,0:T(1,128)S(1)} %get-tuple-element.176) | copy-start | bytes 3076
  92.9 7.6 %copy-start.47 = (f32[1,256]{1,0:T(1,128)}, f32[1,256]{1,0:T(1,128)S(1)}, u32[]{:S(2)}) copy-start(f32[1,256]{1,0:T(1,128)S(1)} %get-tuple-element.179) | copy-start | bytes 3076
  93.6 22.4 %copy-start.56 = (pred[2,2]{1,0:T(4,128)(4,1)S(1)}, pred[2,2]{1,0:T(4,128)(4,1)}, u32[]{:S(2)}) copy-start(pred[2,2]{1,0:T(4,128)(4,1)} %iota_compare_fusion.2) | copy-start | bytes 16
  101.4 24.6 %copy-start.34 = (f32[2,8,8,128]{3,2,1,0:T(8,128)S(1)}, f32[2,8,8,128]{3,2,1,0:T(8,128)}, u32[]{:S(2)}) copy-start(f32[2,8,8,128]{3,2,1,0:T(8,128)} %convolution_bitcast_fusion.2) | copy-start | bytes 196612
  108.6 23.6 %copy-start.49 = (f32[1,512]{1,0:T(1,128)S(1)}, f32[1,512]{1,0:T(1,128)}, u32[]{:S(2)}) copy-start(f32[1,512]{1,0:T(1,128)} %get-tuple-element.183) | copy-start | bytes 6148
  108.7 23.6 %copy-start.50 = (f32[1,512]{1,0:T(1,128)S(1)}, f32[1,512]{1,0:T(1,128)}, u32[]{:S(2)}) copy-start(f32[1,512]{1,0:T(1,128)} %get-tuple-element.184) | copy-start | bytes 6148
  109.9 7.2 %all-to-all-start.2 = ((f32[8,1,128]{2,1,0:T(1,128)}), f32[8,1,128]{2,1,0:T(1,128)S(1)}, u32[]{:S(2)}, u32[]{:S(2)}) async-start(f32[8,1,128]{2,1,0:T(1,128)} %reshape.561), calls=%async_computation.2 | async-start | bytes 8192 | tf_op jit(solution)/shard_map/all_to_all | solution.py:466
  117.1 356.8 %all-to-all-start = ((f32[1,2,8,64,128]{4,2,1,0,3:T(8,128)}), f32[1,2,8,64,128]{4,2,1,0,3:T(8,128)}, u32[]{:S(2)}, u32[]{:S(2)}) async-start(f32[1,2,8,64,128]{4,2,1,0,3:T(8,128)} %copy.321), calls=%async_computation | async-start | bytes 1048576 | tf_op jit(solution)/shard_map/all_to_all | solution.py:467
  134.3 26.2 %copy-start.7 = (f32[512,512]{0,1:T(8,128)}, f32[512,512]{0,1:T(8,128)S(1)}, u32[]{:S(2)}) copy-start(f32[512,512]{0,1:T(8,128)S(1)} %divide_multiply_fusion.1) | copy-start | bytes 3145732
  134.3 3.2 copy-start.25
  134.3 3.2 copy-start.26
  134.3 3.2 copy-start.27
  134.4 3.2 copy-start.28
  137.6 26.2 %copy-start.13 = (f32[64,512]{1,0:T(8,128)S(1)}, f32[64,512]{1,0:T(8,128)}, u32[]{:S(2)}) copy-start(f32[64,512]{1,0:T(8,128)} %param.20) | copy-start | bytes 393220
  160.5 3.3 copy-start.6
  191.2 12.2 %copy-start.2 = (f32[2,32,64,256]{3,2,1,0:T(8,128)S(1)}, f32[2,32,64,256]{3,2,1,0:T(8,128)}, u32[]{:S(2)}) copy-start(f32[2,32,64,256]{3,2,1,0:T(8,128)} %get-tuple-element.273) | copy-start | bytes 12582916 | tf_op jit(solution)/shard_map/vmap()/while
  203.5 4.1 copy-start.5
  224.6 12.2 %copy-start.2 = (f32[2,32,64,256]{3,2,1,0:T(8,128)S(1)}, f32[2,32,64,256]{3,2,1,0:T(8,128)}, u32[]{:S(2)}) copy-start(f32[2,32,64,256]{3,2,1,0:T(8,128)} %get-tuple-element.273) | copy-start | bytes 12582916 | tf_op jit(solution)/shard_map/vmap()/while
  236.8 4.3 copy-start.5
  246.0 4.8 copy-start.4
  246.0 205.8 %slice-start = ((s8[8388608]{0:T(1024)(128)(4,1)}), s8[4194304]{0:T(1024)(128)(4,1)S(1)}, s32[]{:S(2)}) async-start(s8[8388608]{0:T(1024)(128)(4,1)} %bitcast.282), calls=%async_computation.4 | async-start | bytes 8388608
  250.7 195.0 %copy-start.8 = (f32[512,512]{0,1:T(8,128)S(1)}, f32[512,512]{0,1:T(8,128)}, u32[]{:S(2)}) copy-start(f32[512,512]{0,1:T(8,128)} %copy-done.7) | copy-start | bytes 3145732
  250.7 195.0 %copy-start.11 = (f32[2,32,512]{2,1,0:T(8,128)S(1)}, f32[2,32,512]{2,1,0:T(8,128)}, u32[]{:S(2)}) copy-start(f32[2,32,512]{2,1,0:T(8,128)} %exp.113) | copy-start | bytes 393220
  445.7 6.0 %slice-start.1 = ((s8[8388608]{0:T(1024)(128)(4,1)}), s8[4194304]{0:T(1024)(128)(4,1)S(1)}, s32[]{:S(2)}) async-start(s8[8388608]{0:T(1024)(128)(4,1)} %bitcast.282), calls=%async_computation.5 | async-start | bytes 8388608
  445.7 6.0 %copy-start.36 = (f32[4096]{0:T(1024)S(1)}, f32[4096]{0:T(1024)}, u32[]{:S(2)}) copy-start(f32[4096]{0:T(1024)} %mul.682) | copy-start | bytes 49156
  457.0 6.4 %copy-start.9 = (f32[1,2048]{0,1:T(8,128)S(1)}, f32[1,2048]{0,1:T(8,128)}, u32[]{:S(2)}) copy-start(f32[1,2048]{0,1:T(8,128)} %copy.372) | copy-start | bytes 24580
  463.4 5.9 %copy-start.15 = (f32[1,256]{0,1:T(8,128)S(1)}, f32[1,256]{0,1:T(8,128)}, u32[]{:S(2)}) copy-start(f32[1,256]{0,1:T(8,128)} %copy.361) | copy-start | bytes 3076
  467.4 3.6 copy-start.29
  467.4 3.6 copy-start.30
  467.4 3.6 copy-start.46
  467.4 3.6 copy-start.48
  467.4 3.6 copy-start.51
  467.4 3.6 copy-start.52
  467.4 3.8 copy-start.38
  467.4 3.8 copy-start.44
  467.5 5.1 %copy-start.18 = (f32[1,8,32,64]{3,2,1,0:T(8,128)S(1)}, f32[1,8,32,64]{3,2,1,0:T(8,128)}, u32[]{:S(2)}) copy-start(f32[1,8,32,64]{3,2,1,0:T(8,128)} %squeeze.26) | copy-start | bytes 196612
  467.5 5.1 %copy-start.19 = (f32[1,8,32,64]{3,2,1,0:T(8,128)S(1)}, f32[1,8,32,64]{3,2,1,0:T(8,128)}, u32[]{:S(2)}) copy-start(f32[1,8,32,64]{3,2,1,0:T(8,128)} %squeeze.28) | copy-start | bytes 196612
  467.5 5.1 %copy-start.31 = (f32[8,32]{0,1:T(8,128)S(1)}, f32[8,32]{0,1:T(8,128)}, u32[]{:S(2)}) copy-start(f32[8,32]{0,1:T(8,128)} %copy.309) | copy-start | bytes 3076
  467.5 5.1 %copy-start.32 = (f32[32,64]{1,0:T(8,128)S(1)}, f32[32,64]{1,0:T(8,128)}, u32[]{:S(2)}) copy-start(f32[32,64]{1,0:T(8,128)} %mul.729) | copy-start | bytes 24580
  467.5 5.1 %copy-start.33 = (f32[32,64]{1,0:T(8,128)S(1)}, f32[32,64]{1,0:T(8,128)}, u32[]{:S(2)}) copy-start(f32[32,64]{1,0:T(8,128)} %mul.691) | copy-start | bytes 24580
  467.5 5.1 %copy-start.58 = (f32[32]{0:T(128)S(1)}, f32[32]{0:T(128)}, u32[]{:S(2)}) copy-start(f32[32]{0:T(128)} %dynamic_slice.76) | copy-start | bytes 388
  467.6 6.3 %copy-start.20 = (f32[8,2,8,8]{3,0,2,1:T(8,128)S(1)}, f32[8,2,8,8]{3,0,2,1:T(8,128)}, u32[]{:S(2)}) copy-start(f32[8,2,8,8]{3,0,2,1:T(8,128)} %get-tuple-element.157) | copy-start | bytes 12292
  467.6 8.4 %copy-start.1 = (bf16[2,8,8192]{2,1,0:T(8,128)(2,1)S(1)}, bf16[2,8,8192]{2,1,0:T(8,128)(2,1)}, u32[]{:S(2)}) copy-start(bf16[2,8,8192]{2,1,0:T(8,128)(2,1)} %param.28) | copy-start | bytes 786436
  469.3 5.8 %copy-start.35 = (f32[8,8,128,2]{2,3,1,0:T(2,128)S(1)}, f32[8,8,128,2]{2,3,1,0:T(2,128)}, u32[]{:S(2)}) copy-start(f32[8,8,128,2]{2,3,1,0:T(2,128)} %fusion.94) | copy-start | bytes 196612
  469.3 5.8 %copy-start.41 = (f32[2,8,8]{2,1,0:T(8,128)S(1)}, f32[2,8,8]{2,1,0:T(8,128)}, u32[]{:S(2)}) copy-start(f32[2,8,8]{2,1,0:T(8,128)} %get-tuple-element.154) | copy-start | bytes 1540
  469.4 5.8 %copy-start.42 = (f32[2,8,8]{2,1,0:T(8,128)S(1)}, f32[2,8,8]{2,1,0:T(8,128)}, u32[]{:S(2)}) copy-start(f32[2,8,8]{2,1,0:T(8,128)} %get-tuple-element.155) | copy-start | bytes 1540
  (7 other events, 10.9 us)
Sparse Core Ops, SparseCore 0:
  63.2 206.4 all-reduce.2

commit v2 on v1

--- a/solution.py
+++ b/solution.py
@@ -22,17 +22,13 @@
 HIGH = lax.Precision.HIGH
 MESH = pl.DeviceIdType.MESH
 NEG = -1e30
+PAIR = 2 * HDIM
 
 
 def passed_along(value, axis, steps):
     count = lax.axis_size(axis)
     first, last = (max(0, -steps), min(count, count - steps))
     return lax.ppermute(value, axis, [(source, source + steps) for source in range(first, last)])
-
-
-def from_root(value, axis, source):
-    kept = jnp.where(lax.axis_index(axis) == source, value, 0).astype(value.dtype)
-    return lax.psum(kept, axis)
 
 
 def causal_conv(leading, source, kernel):
@@ -59,40 +55,8 @@
     return jnp.stack(results)
 
 
-def span_pass(ssm_state, block):
-    inputs, entries, readout, log_decay = block
-    cumulative = jnp.cumsum(log_decay, axis=1)
-    block_size = log_decay.shape[1]
-    causal = jnp.arange(block_size)[:, None] >= jnp.arange(block_size)[None, :]
-    spreads = cumulative[:, :, None] - cumulative[:, None, :]
-    weights = jnp.where(causal[None], jnp.exp(jnp.where(causal[None], spreads, 0.0)), 0.0)
-    intersection = jnp.dot(readout, entries.T, precision=HIGH)
-    intra_span = jnp.einsum("kts,skp->tkp", weights * intersection[None], inputs, precision=HIGH)
-    carried = jnp.exp(cumulative).T[:, :, None] * jnp.einsum(
-        "tn,kpn->tkp", readout, ssm_state, precision=HIGH
-    )
-    remaining = jnp.exp(cumulative[:, -1:] - cumulative)
-    updates = jnp.einsum("skp,sn->kpn", inputs * remaining.T[:, :, None], entries, precision=HIGH)
-    renewed = jnp.exp(cumulative[:, -1])[:, None, None] * ssm_state + updates
-    return (renewed, intra_span + carried)
-
-
-def run_spans(inputs, entries, readout, log_decay, ssm_state):
-    row_total, heads_here, head_width = inputs.shape
-    block_total = row_total // SPAN
-    blocks = (
-        inputs.reshape(block_total, SPAN, heads_here, head_width),
-        entries.reshape(block_total, SPAN, entries.shape[1]),
-        readout.reshape(block_total, SPAN, readout.shape[1]),
-        log_decay.reshape(heads_here, block_total, SPAN).transpose(1, 0, 2),
-    )
-    ssm_state, results = lax.scan(span_pass, ssm_state, blocks)
-    return (results.reshape(row_total, heads_here, head_width), ssm_state)
-
-
-def decode_mamba(ssm_state, heads_x, heads_b, heads_c, step_dt, rates, gains):
+def decode_mamba(from_prefix, heads_x, heads_b, heads_c, step_dt, rates, gains):
     decays = jnp.exp(-step_dt * rates)
-    from_prefix = jnp.einsum("jrhn,hpn->jrhp", heads_c, ssm_state, precision=HIGH)
     results = []
     for current in range(heads_x.shape[0]):
         factor = jnp.ones(decays.shape[1:], jnp.float32)
@@ -115,15 +79,46 @@
     return (head_begin // per_group, group_count, head_count // group_count)
 
 
+def split(value):
+    hi = value.astype(jnp.bfloat16)
+    return hi, (value - hi.astype(jnp.float32)).astype(jnp.bfloat16)
+
+
+def split_outside(value):
+    hi = lax.reduce_precision(value, 8, 7)
+    return hi.astype(jnp.bfloat16), (value - hi).astype(jnp.bfloat16)
+
+
+def dot_split(hi, lo, right):
+    right_hi, right_lo = split(right)
+    width = right.shape[1]
+    both = jnp.dot(
+        hi,
+        jnp.concatenate([right_hi, right_lo], axis=1),
+        preferred_element_type=jnp.float32,
+    )
+    small = jnp.dot(lo, right_hi, preferred_element_type=jnp.float32)
+    return both[:, :width] + (both[:, width:] + small)
+
+
 def relay_kernel(
     count,
     groups,
-    chunk,
-    factor_ref,
-    local_ref,
+    x_ref,
+    lead_ref,
+    taps_ref,
+    rows_ref,
+    lanes_ref,
+    bt_hi_ref,
+    bt_lo_ref,
+    c_hi_ref,
+    c_lo_ref,
+    cb_ref,
+    y_ref,
+    prefix_ref,
     incoming_ref,
-    prefix_ref,
     leaving,
+    padded,
     send_sem,
     recv_sem,
     final_send,
@@ -132,11 +127,12 @@
 ):
     me = lax.axis_index("seq")
     mine = lax.axis_index("grp")
-    local_heads = local_ref.shape[0]
-    state_heads = prefix_ref.shape[0]
-    shares = local_heads // state_heads
-    pieces = local_heads // chunk
-    own_pieces = state_heads // chunk
+    pieces = leaving.shape[0]
+    own_pieces = prefix_ref.shape[0]
+    shares = pieces // own_pieces
+    group_pieces = pieces // cb_ref.shape[0]
+    spans = cb_ref.shape[1]
+    section = x_ref.shape[0]
     last = count - 1
     is_last = me == last
     is_root = me // shares == mine
@@ -181,7 +177,7 @@
     pl.semaphore_wait(barrier, expected)
 
     def pass_on(piece, target):
-        rows = pl.ds(piece * chunk, chunk)
+        rows = pl.ds(piece, 1)
         return pltpu.make_async_remote_copy(
             src_ref=leaving.at[rows],
             dst_ref=incoming_ref.at[rows],
@@ -193,8 +189,8 @@
 
     def final_copy(piece, own_piece, owner):
         return pltpu.make_async_remote_copy(
-            src_ref=leaving.at[pl.ds(piece * chunk, chunk)],
-            dst_ref=prefix_ref.at[pl.ds(own_piece * chunk, chunk)],
+            src_ref=leaving.at[pl.ds(piece, 1)],
+            dst_ref=prefix_ref.at[pl.ds(own_piece, 1)],
             send_sem=final_send.at[piece],
             recv_sem=prefix_recv.at[own_piece],
             device_id=(owner, mine),
@@ -202,7 +198,7 @@
         )
 
     def fan_copy(own_piece, other):
-        rows = pl.ds(own_piece * chunk, chunk)
+        rows = pl.ds(own_piece, 1)
         return pltpu.make_async_remote_copy(
             src_ref=prefix_ref.at[rows],
             dst_ref=prefix_ref.at[rows],
@@ -212,20 +208,62 @@
             device_id_type=MESH,
         )
 
+    left_half = lax.broadcasted_iota(jnp.int32, (SPAN, PAIR), 1) < HDIM
+    causal = lax.broadcasted_iota(jnp.int32, (SPAN, SPAN), 0) >= lax.broadcasted_iota(
+        jnp.int32, (SPAN, SPAN), 1
+    )
+
     def one_piece(piece, carry):
-        rows = pl.ds(piece * chunk, chunk)
+        group = piece // group_pieces
+        columns = pl.ds(pl.multiple_of(piece * PAIR, PAIR), PAIR)
+        padded[0:8] = lead_ref[:, columns]
+        padded[8 : 8 + section] = x_ref[:, columns].astype(jnp.float32)
+        taps = taps_ref[:, columns]
+        row_data = rows_ref[piece]
+        column_data = row_data.T
+        lane_data = lanes_ref[piece]
+        gain = lane_data[0:1]
+        factor = lane_data[1:2]
+        convolved = []
+        scaled = []
+        growth = []
+        updates = []
+        for span in range(spans):
+            first = span * SPAN
+            total = jnp.zeros((SPAN, PAIR), jnp.float32)
+            for position in range(TAPS):
+                start = 8 - (TAPS - 1) + first + position
+                total = total + taps[position : position + 1] * padded[start : start + SPAN]
+            value = total / (1.0 + jnp.exp(-total))
+            cols = column_data[first : first + SPAN]
+            level = jnp.where(left_half, cols[:, 0:1], cols[:, 1:2])
+            step = jnp.where(left_half, cols[:, 2:3], cols[:, 3:4])
+            closing = lane_data[2 + span : 3 + span]
+            inputs = value * step
+            convolved.append(value)
+            scaled.append(inputs)
+            growth.append(jnp.exp(level))
+            updates.append(
+                dot_split(
+                    bt_hi_ref[group, :, first : first + SPAN],
+                    bt_lo_ref[group, :, first : first + SPAN],
+                    inputs * jnp.exp(closing - level),
+                )
+            )
+        ending = updates[0]
+        for span in range(1, spans):
+            ending = jnp.exp(lane_data[2 + span : 3 + span]) * ending + updates[span]
 
         @pl.when(me == 0)
         def _():
-            incoming_ref[rows] = jnp.zeros((chunk,) + local_ref.shape[1:], jnp.float32)
+            incoming_ref[piece] = jnp.zeros((STATE, PAIR), jnp.float32)
 
         @pl.when(me > 0)
         def _():
             pass_on(piece, me).wait_recv()
 
-        for head in range(chunk):
-            at = piece * chunk + head
-            leaving[at] = factor_ref[at] * incoming_ref[at] + local_ref[at]
+        state = incoming_ref[piece]
+        leaving[piece] = factor * state + ending
 
         @pl.when(me < last)
         def _():
@@ -240,10 +278,29 @@
 
         @pl.when(jnp.logical_and(is_last, owner == last))
         def _():
-            prefix_ref[pl.ds(own_piece * chunk, chunk)] = leaving[rows]
+            prefix_ref[own_piece] = leaving[piece]
             for other in range(1, groups):
                 fan_copy(own_piece, other).start()
 
+        for span in range(spans):
+            first = span * SPAN
+            carried = growth[span] * dot_split(
+                c_hi_ref[group, first : first + SPAN], c_lo_ref[group, first : first + SPAN], state
+            )
+            halves = []
+            for half in range(2):
+                fall = (
+                    column_data[first : first + SPAN, half : half + 1]
+                    - row_data[half : half + 1, first : first + SPAN]
+                )
+                weights = jnp.exp(jnp.where(causal, fall, NEG)) * cb_ref[group, span]
+                hi, lo = split(weights)
+                halves.append(dot_split(hi, lo, scaled[span]))
+            inside = jnp.where(left_half, halves[0], halves[1])
+            y_ref[first : first + SPAN, columns] = (
+                inside + carried + gain * convolved[span]
+            ).astype(y_ref.dtype)
+            state = jnp.exp(lane_data[2 + span : 3 + span]) * state + updates[span]
         return carry
 
     lax.fori_loop(0, pieces, one_piece, 0)
@@ -287,22 +344,22 @@
         lax.fori_loop(0, own_pieces, drain_fan, 0)
 
 
-def relay_states(factor, local_state, state_heads, count, groups):
-    local_heads = local_state.shape[0]
-    chunk = 2
-    pieces = local_heads // chunk
-    own_pieces = state_heads // chunk
+def relay_states(operands, own_pieces, count, groups):
+    section, width = operands[0].shape
+    pieces = width // PAIR
     vmem = pl.BlockSpec(memory_space=pltpu.VMEM)
     return pl.pallas_call(
-        functools.partial(relay_kernel, count, groups, chunk),
+        functools.partial(relay_kernel, count, groups),
         out_shape=(
-            jax.ShapeDtypeStruct(local_state.shape, jnp.float32),
-            jax.ShapeDtypeStruct((state_heads,) + local_state.shape[1:], jnp.float32),
+            jax.ShapeDtypeStruct((section, width), jnp.bfloat16),
+            jax.ShapeDtypeStruct((own_pieces, STATE, PAIR), jnp.float32),
         ),
-        in_specs=[pl.BlockSpec(memory_space=pltpu.SMEM), vmem],
+        in_specs=[vmem] * len(operands),
         out_specs=(vmem, vmem),
         scratch_shapes=[
-            pltpu.VMEM(local_state.shape, jnp.float32),
+            pltpu.VMEM((pieces, STATE, PAIR), jnp.float32),
+            pltpu.VMEM((pieces, STATE, PAIR), jnp.float32),
+            pltpu.VMEM((section + 8, PAIR), jnp.float32),
             pltpu.SemaphoreType.DMA((pieces,)),
             pltpu.SemaphoreType.DMA((pieces,)),
             pltpu.SemaphoreType.DMA((pieces,)),
@@ -310,9 +367,9 @@
             pltpu.SemaphoreType.DMA((groups - 1, own_pieces)),
         ],
         compiler_params=pltpu.CompilerParams(
-            collective_id=0, has_side_effects=True, vmem_limit_bytes=40 * 1024 * 1024
+            collective_id=0, has_side_effects=True, vmem_limit_bytes=48 * 1024 * 1024
         ),
-    )(factor, local_state)
+    )(*operands)
 
 
 def on_device(
@@ -342,20 +399,20 @@
     c_offset = HEADS * HDIM + GROUPS * STATE
     head_begin = grp_index * local_heads
     group_begin, group_count, heads_each = group_layout(head_begin, local_heads)
-    source_x = pre_x.astype(jnp.float32)
+    last_x = pre_x[section - edge :].astype(jnp.float32)
     full_b = pre_b.astype(jnp.float32)
     full_c = pre_c.astype(jnp.float32)
     own_b = lax.dynamic_slice_in_dim(full_b, group_begin * STATE, group_count * STATE, 1)
     own_c = lax.dynamic_slice_in_dim(full_c, group_begin * STATE, group_count * STATE, 1)
     edge_rows = jnp.concatenate(
-        [source_x[section - edge :], own_b[section - edge :], own_c[section - edge :]], axis=1
+        [last_x, own_b[section - edge :], own_c[section - edge :]], axis=1
     )
     edge_rows = passed_along(edge_rows, "seq", 1)
     split_b = local_heads * HDIM
     split_c = split_b + group_count * STATE
     leading = (edge_rows[:, :split_b], edge_rows[:, split_b:split_c], edge_rows[:, split_c:])
     is_end = seq_index == seq_count - 1
-    shown_x = jnp.where(is_end, source_x[section - edge :], 0.0)
+    shown_x = jnp.where(is_end, last_x, 0.0)
     shown_bc = jnp.where(
         jnp.logical_and(is_end, grp_index == 0),
         jnp.concatenate([full_b[section - edge :], full_c[section - edge :]], axis=1),
@@ -371,37 +428,55 @@
     kernel_c = lax.dynamic_slice_in_dim(
         conv_taps, c_offset + group_begin * STATE, group_count * STATE, 1
     )
-    conv_x = causal_conv(leading[0], source_x, kernel_x)
     conv_b = causal_conv(leading[1], own_b, kernel_b)
     conv_c = causal_conv(leading[2], own_c, kernel_c)
     rates = lax.dynamic_slice_in_dim(decay_rate, head_begin, local_heads, 0)
     gains = lax.dynamic_slice_in_dim(skip_gain, head_begin, local_heads, 0)
-    log_decay = -pre_dt * rates[:, None]
-    head_inputs = conv_x.reshape(section, local_heads, HDIM)
-    scaled = head_inputs * pre_dt.T[:, :, None]
-    grouped = scaled.reshape(section, group_count, heads_each, HDIM).transpose(1, 0, 2, 3)
-    entries = conv_b.reshape(section, group_count, STATE).transpose(1, 0, 2)
+    spans = section // SPAN
+    pieces = local_heads // 2
+    log_decay = (-pre_dt * rates[:, None]).reshape(local_heads, spans, SPAN)
+    levels = jnp.cumsum(log_decay, axis=2)
+    closings = levels[:, :, -1]
+    row_data = jnp.concatenate(
+        [
+            levels.reshape(pieces, 2, section),
+            pre_dt.reshape(pieces, 2, section),
+            jnp.zeros((pieces, 4, section), jnp.float32),
+        ],
+        axis=1,
+    )
+    lane_data = jnp.concatenate(
+        [gains[:, None], jnp.exp(jnp.sum(closings, axis=1))[:, None], closings], axis=1
+    )
+    lane_data = jnp.repeat(
+        lane_data.reshape(pieces, 2, spans + 2).transpose(0, 2, 1), HDIM, axis=2
+    )
+    lane_data = jnp.pad(lane_data, ((0, 0), (0, 6 - spans), (0, 0)))
+    entries = conv_b.reshape(section, group_count, STATE).transpose(1, 2, 0)
     readout = conv_c.reshape(section, group_count, STATE).transpose(1, 0, 2)
-    decay_groups = log_decay.reshape(group_count, heads_each, section)
-    blank = jnp.zeros((group_count, heads_each, HDIM, STATE), jnp.float32)
-    intra_part, closing_local = jax.vmap(run_spans)(grouped, entries, readout, decay_groups, blank)
-    local_state = closing_local.reshape(local_heads, HDIM, STATE)
-    cumulative = jnp.cumsum(log_decay, axis=1)
-    section_decay = cumulative[:, -1]
-
+    crossing = jnp.einsum(
+        "gitn,gnis->gits",
+        readout.reshape(group_count, spans, SPAN, STATE),
+        entries.reshape(group_count, STATE, spans, SPAN),
+        precision=HIGH,
+    )
     state_heads = HEADS // seq_count
-    incoming, prefix_state = relay_states(
-        jnp.exp(section_decay), local_state, state_heads, seq_count, lax.axis_size("grp")
-    )
-    incoming_groups = incoming.reshape(group_count, heads_each, HDIM, STATE)
-    from_before = jnp.einsum("gsn,gkpn->gskp", readout, incoming_groups, precision=HIGH)
-    decay_factor = jnp.exp(cumulative).reshape(group_count, heads_each, section).transpose(0, 2, 1)
-    combined = intra_part + decay_factor[..., None] * from_before
-    combined = (
-        combined.transpose(1, 0, 2, 3).reshape(section, local_heads, HDIM)
-        + gains[None, :, None] * head_inputs
-    )
-    pre_y = combined.reshape(section, local_heads * HDIM).astype(jnp.bfloat16)
+    own_pieces = state_heads // 2
+    pre_y, prefix_pairs = relay_states(
+        (
+            pre_x,
+            jnp.pad(leading[0], ((8 - edge, 0), (0, 0))),
+            jnp.pad(kernel_x, ((0, 8 - TAPS), (0, 0))),
+            row_data,
+            lane_data,
+            *split_outside(entries),
+            *split_outside(readout),
+            crossing,
+        ),
+        own_pieces,
+        seq_count,
+        lax.axis_size("grp"),
+    )
     prefix_tail = lax.dynamic_slice_in_dim(
         tails, seq_index * state_heads * HDIM, state_heads * HDIM, 1
     )
@@ -437,7 +512,13 @@
     heads_c = jnp.repeat(step_c.reshape(STEPS, rows_here, dgroup_count, STATE), dheads_each, axis=2)
     dec_rates = lax.dynamic_slice_in_dim(decay_rate, dec_begin, state_heads, 0)
     dec_gains = lax.dynamic_slice_in_dim(skip_gain, dec_begin, state_heads, 0)
-    mamba_out = decode_mamba(prefix_state, heads_x, heads_b, heads_c, dec_dt, dec_rates, dec_gains)
+    from_prefix = jnp.einsum(
+        "jrgn,gqnl->jrgql",
+        step_c.reshape(STEPS, rows_here, dgroup_count, STATE),
+        prefix_pairs.reshape(dgroup_count, own_pieces // dgroup_count, STATE, PAIR),
+        precision=HIGH,
+    ).reshape(STEPS, rows_here, state_heads, HDIM)
+    mamba_out = decode_mamba(from_prefix, heads_x, heads_b, heads_c, dec_dt, dec_rates, dec_gains)
     dec_y = mamba_out.reshape(STEPS, rows_here, state_heads * HDIM).astype(jnp.bfloat16)
     group_size = QHEADS // KVHEADS
     score_scale = ADIM ** (-0.5)

time: 489 us -> 299 us (0.61)
  local copies, waits for them, and re-layouts: 123 us -> 35.6 us
  other arithmetic: 76 us -> 29.4 us
  matrix products: 51.1 us -> 8.01 us
    dot_general x9 -> x2, matrix products: 44.8 us -> 1.23 us  [the longest x1 0.63 us: on_device(): jnp.einsum('gitn,gnis->gits', readout.reshape(group_count, spans, SPAN, S...]
    unnamed x141 -> x71, local copies, waits for them, and re-layouts: 35.9 us -> 7.43 us
    mul x3 -> x2, other arithmetic: 27.5 us -> 3.88 us  [causal_conv(): return jax.nn.silu(accumulated)]
    dynamic_slice x4 -> x1, local copies, waits for them, and re-layouts: 19.9 us -> 1.47 us  [on_device(): lax.dynamic_slice_in_dim(conv_taps, head_begin * HDIM, local_heads * HDIM...]
    reshape x4 -> x5, local copies, waits for them, and re-layouts: 15.3 us -> 1.88 us  [the longest x1 1.56 us: on_device(): readout = conv_c.reshape(section, group_count, STATE).transpose(1, 0, 2)]
    slice x11 -> x2, local copies, waits for them, and re-layouts: 12.3 us -> 0.19 us  [the longest x2 5.1 us: on_device(): source_x[section - edge:]]
    convert_element_type x2 -> x4, other arithmetic: 11.9 us -> 1.18 us  [the longest x1 0.86 us: on_device(): last_x = pre_x[section - edge:].astype(jnp.float32)]
    concatenate x1, local copies, waits for them, and re-layouts: 6.77 us -> 0.78 us  [on_device(): jnp.concatenate([jnp.zeros((edge, x_offset), jnp.float32), shown_bc], axi...]
  transfers between devices with their start and end apart: 5 -> 5, of which waited for: 1 -> 0; matrix products, arithmetic and copies ran while one was open for 49% -> 21% of each run, Pallas kernels for 40% -> 64%
where the time goes in v2:
time: 299 us; the launch traced here: 297 us
  Pallas kernels  191 us (64%)
  local copies, waits for them, and re-layouts  35.6 us (12%)
  other arithmetic  29.4 us (10%)
  starting transfers between devices  18.6 us (6%)
  between operations  14.9 us (5%)
  matrix products  8.01 us (3%)
    pallas_call x1, Pallas kernels, relay_states(): pl.pallas_call(functools.partial(relay_kernel, count, groups), out_shape=...  191 us
    unnamed x71, local copies, waits for them, and re-layouts  7.43 us
  transfers between devices with their start and end apart: 5, of which 0 were waited for; matrix products, arithmetic and copies ran while one was open for 21% of the time, Pallas kernels for 64%

profile of v2, /device:TPU:25, one launch (start us, length us, event | category | flops | bytes accessed | tf_op | source)
XLA Modules:
  0.0 297.4 jit_solution(743510713851675336)
XLA Ops:
  7.2 1.8 fusion.76
  9.0 0.3 copy.162
  9.4 0.3 copy-done.27
  9.7 1.5 fusion.79
  11.4 0.7 reshape.441
  12.1 5.5 %all-to-all-start.1 = ((f32[8,1,128]{2,1,0:T(1,128)}), f32[8,1,128]{2,1,0:T(1,128)}, u32[]{:S(2)}, u32[]{:S(2)}) async-start(f32[8,1,128]{2,1,0:T(1,128)} %reshape.441), calls=%async_computation.1 | async-start | bytes 8192 | tf_op jit(solution)/shard_map/all_to_all | solution.py:546
  17.6 0.8 slice.313
  18.4 0.8 concatenate.36
  19.2 1.5 select_dynamic-update-slice_fusion
  20.8 0.8 dynamic-slice.1
  21.6 0.9 slice_convert_fusion
  22.5 0.7 pad_maximum_fusion.2
  23.1 3.1 %collective-permute-start = (f32[3,5120]{1,0:T(4,128)}, f32[3,5120]{1,0:T(4,128)}, u32[]{:S(2)}, u32[]{:S(2)}) collective-permute-start(f32[3,5120]{1,0:T(4,128)} %pad_maximum_fusion.2), channel_id=1, source_target_pairs={{0,4},{4,8},{8,12},{12,16},{16,20},{20,24},{24,28},{1,5},{5,9},{9,... | collective-permute-start | bytes 184328 | tf_op jit(solution)/shard_map/ppermute | solution.py:31
  26.3 2.5 convert_element_type.47
  28.7 2.5 convert_element_type.48
  31.6 1.2 reduce-window.6
  33.4 1.1 fusion.33
  34.5 0.3 copy.163
  34.9 0.7 convolution_bitcast_fusion
  35.7 0.2 slice_reduce_fusion.1
  36.7 0.8 reduce_window_sum.20
  37.5 1.5 constant_dynamic-slice_fusion.6
  39.0 0.6 slice_bitcast_fusion.5
  39.6 1.9 fusion.8
  41.5 0.8 convolution_bitcast_fusion.1
  42.4 1.7 constant_dynamic-slice_fusion.7
  44.2 1.3 dynamic-slice_convert_fusion
  45.5 1.0 maximum_maximum_fusion.rows_ref
  46.6 1.6 constant_dynamic-slice_fusion.5
  48.1 0.6 maximum_bitcast_fusion.2
  48.7 0.6 dynamic_slice.61
  49.3 0.9 copy.138
  50.4 1.0 copy.157
  51.4 0.7 reshape.443
  52.2 1.1 copy.131
  54.1 0.7 mul.531
  54.9 4.5 %all-to-all-start.2 = ((f32[8,1,128]{2,1,0:T(1,128)}), f32[8,1,128]{2,1,0:T(1,128)S(1)}, u32[]{:S(2)}, u32[]{:S(2)}) async-start(f32[8,1,128]{2,1,0:T(1,128)} %reshape.443), calls=%async_computation.2 | async-start | bytes 8192 | tf_op jit(solution)/shard_map/all_to_all | solution.py:547
  59.4 0.5 broadcast.278
  59.9 1.3 reduce.10
  61.6 2.0 fusion.75
  63.5 5.4 %all-to-all-start = ((f32[1,2,8,64,128]{4,2,1,0,3:T(8,128)}), f32[1,2,8,64,128]{4,2,1,0,3:T(8,128)}, u32[]{:S(2)}, u32[]{:S(2)}) async-start(f32[1,2,8,64,128]{4,2,1,0,3:T(8,128)} %copy.131), calls=%async_computation | async-start | bytes 1048576 | tf_op jit(solution)/shard_map/all_to_all | solution.py:548
  69.0 0.6 reduce.11
  69.9 1.3 fusion.46
  71.2 0.9 copy.140
  72.1 1.8 fusion.50
  73.9 0.8 multiply_add_fusion.1
  74.7 0.7 fusion.78
  75.4 2.3 divide_multiply_fusion
  77.7 2.5 copy.124
  80.2 1.6 copy.125
  81.8 1.6 divide_multiply_fusion.1
  83.4 1.6 copy.123
  85.2 0.6 fusion.25.cb_ref
  86.0 0.9 slice.298
  86.9 190.9 %shard_map.166 = (bf16[512,4096]{1,0:T(8,128)(2,1)}, f32[16,256,128]{2,1,0:T(8,128)S(1)}) custom-call(bf16[512,4096]{1,0:T(8,128)(2,1)} %x_ref.1, f32[8,4096]{1,0:T(8,128)S(1)} %pad.13.lead_ref, f32[8,4096]{1,0:T(8,128)S(1)} %pad.14.taps_ref, f32[32,8,512]{2,1,0:T(8,128)S(1)} %maximum_maximum_fusion.rows_ref, f32[32,8,128]{2,1,0:T(8,128)S(1)} %pad.15.lanes_ref, ...), custom_call_target="tpu_custom_call" | custom-call | tf_op jit(solution)/shard_map/pallas_call | solution.py:351
  277.9 0.8 fusion.77
  278.7 1.0 fusion.71
  279.8 0.8 bitcast_multiply_fusion.4
  280.6 0.6 fusion.4
  282.0 1.1 fusion.60
  283.2 0.6 pad_maximum_fusion.3
  283.9 1.3 fusion.32
  285.3 0.6 convert_element_type.57
  285.9 4.7 %copy.200 = bf16[512,4096]{1,0:T(8,128)(2,1)} copy(bf16[512,4096]{1,0:T(8,128)(2,1)} %get-tuple-element.70) | data formatting | bytes 8388608
  (137 shorter events, 5.3 us)
Async XLA Ops:
  7.2 2.6 copy-start
  9.0 0.7 copy-start.27
  9.3 8.3 %copy-start.1 = (bf16[512,2048]{1,0:T(8,128)(2,1)S(1)}, bf16[512,2048]{1,0:T(8,128)(2,1)}, u32[]{:S(2)}) copy-start(bf16[512,2048]{1,0:T(8,128)(2,1)} %param.16) | copy-start | bytes 6291460
  11.3 17.5 %copy-start.5 = (f32[2,8,8,8]{3,0,2,1:T(2,128)}, f32[2,8,8,8]{3,0,2,1:T(2,128)S(1)}, u32[]{:S(2)}) copy-start(f32[2,8,8,8]{3,0,2,1:T(2,128)S(1)} %get-tuple-element.61) | copy-start | bytes 12292
  12.1 42.8 %all-to-all-start.1 = ((f32[8,1,128]{2,1,0:T(1,128)}), f32[8,1,128]{2,1,0:T(1,128)}, u32[]{:S(2)}, u32[]{:S(2)}) async-start(f32[8,1,128]{2,1,0:T(1,128)} %reshape.441), calls=%async_computation.1 | async-start | bytes 8192 | tf_op jit(solution)/shard_map/all_to_all | solution.py:546
  17.6 260.3 %all-reduce.6.cloned.1.call-start = ((), (), s32[]{:S(2)}) async-start(), calls=%async_computation.3 | async-start | bytes 655360 | tf_op jit(solution)/shard_map/psum | solution.py:423
  23.1 51.6 %collective-permute-start = (f32[3,5120]{1,0:T(4,128)}, f32[3,5120]{1,0:T(4,128)}, u32[]{:S(2)}, u32[]{:S(2)}) collective-permute-start(f32[3,5120]{1,0:T(4,128)} %pad_maximum_fusion.2), channel_id=1, source_target_pairs={{0,4},{4,8},{8,12},{12,16},{16,20},{20,24},{24,28},{1,5},{5,9},{9,... | collective-permute-start | bytes 184328 | tf_op jit(solution)/shard_map/ppermute | solution.py:31
  26.2 13.4 %copy-start.25 = (pred[2,2]{1,0:T(4,128)(4,1)}, pred[2,2]{1,0:T(4,128)(4,1)S(1)}, u32[]{:S(2)}) copy-start(pred[2,2]{1,0:T(4,128)(4,1)S(1)} %iota_compare_fusion.1) | copy-start | bytes 16
  26.2 2.5 copy-start.2
  28.7 2.6 copy-start.28
  28.7 2.6 copy-start.4
  31.3 2.1 copy-start.13
  31.3 2.1 copy-start.3
  31.3 2.1 copy-start.6
  34.9 1.5 copy-start.29
  34.9 4.1 %copy-start.18 = (f32[2,8,32]{2,1,0:T(8,128)S(1)}, f32[2,8,32]{2,1,0:T(8,128)}, u32[]{:S(2)}) copy-start(f32[2,8,32]{2,1,0:T(8,128)} %param.25) | copy-start | bytes 6148
  39.0 3.3 %copy-start.15 = (f32[2,8,32]{2,1,0:T(8,128)}, f32[2,8,32]{2,1,0:T(8,128)S(1)}, u32[]{:S(2)}) copy-start(f32[2,8,32]{2,1,0:T(8,128)S(1)} %multiply_exponential_fusion) | copy-start | bytes 6148
  42.4 6.4 %copy-start.30 = (f32[256]{0:T(256)S(1)}, f32[256]{0:T(256)}, u32[]{:S(2)}) copy-start(f32[256]{0:T(256)} %param.20) | copy-start | bytes 3076
  50.4 3.4 %copy-start.7 = (f32[4,4096]{1,0:T(4,128)S(1)}, f32[4,4096]{1,0:T(4,128)}, u32[]{:S(2)}) copy-start(f32[4,4096]{1,0:T(4,128)} %constant_dynamic-slice_fusion.6) | copy-start | bytes 196612
  52.1 1.2 copy-start.20
  52.1 1.7 copy-start.19
  52.1 1.9 copy-start.26
  52.2 2.6 copy-start.10
  54.9 8.7 %all-to-all-start.2 = ((f32[8,1,128]{2,1,0:T(1,128)}), f32[8,1,128]{2,1,0:T(1,128)S(1)}, u32[]{:S(2)}, u32[]{:S(2)}) async-start(f32[8,1,128]{2,1,0:T(1,128)} %reshape.443), calls=%async_computation.2 | async-start | bytes 8192 | tf_op jit(solution)/shard_map/all_to_all | solution.py:547
  61.5 7.4 %copy-start.8 = (f32[2,8,8]{2,1,0:T(8,128)}, f32[2,8,8]{2,1,0:T(8,128)S(1)}, u32[]{:S(2)}) copy-start(f32[2,8,8]{2,1,0:T(8,128)S(1)} %bitcast_reduce_fusion) | copy-start | bytes 1540
  61.6 7.4 %copy-start.9 = (f32[2,8,8]{2,1,0:T(8,128)}, f32[2,8,8]{2,1,0:T(8,128)S(1)}, u32[]{:S(2)}) copy-start(f32[2,8,8]{2,1,0:T(8,128)S(1)} %max.13) | copy-start | bytes 1540
  63.5 220.3 %all-to-all-start = ((f32[1,2,8,64,128]{4,2,1,0,3:T(8,128)}), f32[1,2,8,64,128]{4,2,1,0,3:T(8,128)}, u32[]{:S(2)}, u32[]{:S(2)}) async-start(f32[1,2,8,64,128]{4,2,1,0,3:T(8,128)} %copy.131), calls=%async_computation | async-start | bytes 1048576 | tf_op jit(solution)/shard_map/all_to_all | solution.py:548
  77.7 4.1 %copy-start.21 = (f32[1,512]{1,0:T(1,128)S(1)}, f32[1,512]{1,0:T(1,128)}, u32[]{:S(2)}) copy-start(f32[1,512]{1,0:T(1,128)} %get-tuple-element.46) | copy-start | bytes 6148
  77.7 4.1 %copy-start.22 = (f32[1,512]{1,0:T(1,128)S(1)}, f32[1,512]{1,0:T(1,128)}, u32[]{:S(2)}) copy-start(f32[1,512]{1,0:T(1,128)} %get-tuple-element.47) | copy-start | bytes 6148
  77.7 4.1 %copy-start.23 = (f32[1,512]{1,0:T(1,128)S(1)}, f32[1,512]{1,0:T(1,128)}, u32[]{:S(2)}) copy-start(f32[1,512]{1,0:T(1,128)} %get-tuple-element.48) | copy-start | bytes 6148
  77.7 4.1 %copy-start.24 = (f32[1,512]{1,0:T(1,128)S(1)}, f32[1,512]{1,0:T(1,128)}, u32[]{:S(2)}) copy-start(f32[1,512]{1,0:T(1,128)} %get-tuple-element.50) | copy-start | bytes 6148
  86.9 192.8 %copy-start.11 = (f32[2,8,256]{2,1,0:T(8,128)S(1)}, f32[2,8,256]{2,1,0:T(8,128)}, u32[]{:S(2)}) copy-start(f32[2,8,256]{2,1,0:T(8,128)} %get-tuple-element.65) | copy-start | bytes 49156
  86.9 192.8 %copy-start.12 = (f32[2,8,256]{2,1,0:T(8,128)S(1)}, f32[2,8,256]{2,1,0:T(8,128)}, u32[]{:S(2)}) copy-start(f32[2,8,256]{2,1,0:T(8,128)} %get-tuple-element.66) | copy-start | bytes 49156
  86.9 193.0 %copy-start.16 = (f32[2,8,32]{2,1,0:T(8,128)S(1)}, f32[2,8,32]{2,1,0:T(8,128)}, u32[]{:S(2)}) copy-start(f32[2,8,32]{2,1,0:T(8,128)} %copy-done.15) | copy-start | bytes 6148
  277.8 5.3 %copy-start.17 = (f32[2048]{0:T(1024)S(1)}, f32[2048]{0:T(1024)}, u32[]{:S(2)}) copy-start(f32[2048]{0:T(1024)} %mul.531) | copy-start | bytes 24580
  280.6 4.5 %copy-start.14 = (f32[8,8,128,2]{2,3,1,0:T(2,128)S(1)}, f32[8,8,128,2]{2,3,1,0:T(2,128)}, u32[]{:S(2)}) copy-start(f32[8,8,128,2]{2,3,1,0:T(2,128)} %fusion.50) | copy-start | bytes 196612
Sparse Core Ops, SparseCore 0:
  23.8 211.9 all-reduce.5

commit v3 on v2

--- a/solution.py
+++ b/solution.py
@@ -136,6 +136,8 @@
     last = count - 1
     is_last = me == last
     is_root = me // shares == mine
+    hands_on = lax.rem(me // shares, 2) == lax.rem(mine, 2)
+    sibling = mine + 1 - 2 * lax.rem(mine, 2)
 
     barrier = pltpu.get_barrier_semaphore()
 
@@ -205,6 +207,17 @@
             send_sem=fan_send.at[other - 1, own_piece],
             recv_sem=prefix_recv.at[own_piece],
             device_id=(me, lax.rem(mine + other, groups)),
+            device_id_type=MESH,
+        )
+
+    def sibling_copy(own_piece):
+        rows = pl.ds(own_piece, 1)
+        return pltpu.make_async_remote_copy(
+            src_ref=prefix_ref.at[rows],
+            dst_ref=prefix_ref.at[rows],
+            send_sem=fan_send.at[0, own_piece],
+            recv_sem=prefix_recv.at[own_piece],
+            device_id=(me, sibling),
             device_id_type=MESH,
         )
 
@@ -279,8 +292,9 @@
         @pl.when(jnp.logical_and(is_last, owner == last))
         def _():
             prefix_ref[own_piece] = leaving[piece]
-            for other in range(1, groups):
+            for other in range(2, groups, 2):
                 fan_copy(own_piece, other).start()
+            sibling_copy(own_piece).start()
 
         for span in range(spans):
             first = span * SPAN
@@ -312,8 +326,12 @@
 
         @pl.when(jnp.logical_and(is_root, me < last))
         def _():
-            for other in range(1, groups):
+            for other in range(2, groups, 2):
                 fan_copy(own_piece, other).start()
+
+        @pl.when(jnp.logical_and(hands_on, jnp.logical_not(jnp.logical_and(is_root, is_last))))
+        def _():
+            sibling_copy(own_piece).start()
 
         return carry
 
@@ -337,11 +355,19 @@
     @pl.when(is_root)
     def _():
         def drain_fan(own_piece, carry):
-            for other in range(1, groups):
+            for other in range(2, groups, 2):
                 fan_copy(own_piece, other).wait_send()
             return carry
 
         lax.fori_loop(0, own_pieces, drain_fan, 0)
+
+    @pl.when(hands_on)
+    def _():
+        def drain_sibling(own_piece, carry):
+            sibling_copy(own_piece).wait_send()
+            return carry
+
+        lax.fori_loop(0, own_pieces, drain_sibling, 0)
 
 
 def relay_states(operands, own_pieces, count, groups):
@@ -542,11 +568,14 @@
     summed_local = summed_local.reshape(STEPS, rows_here, QHEADS, ADIM)
     own_heads = QHEADS // seq_count
     head_start = seq_index * own_heads
-    pieces = (
-        lax.all_to_all(peak_local[None], "seq", split_axis=3, concat_axis=0, tiled=True),
-        lax.all_to_all(mass_local[None], "seq", split_axis=3, concat_axis=0, tiled=True),
-        lax.all_to_all(summed_local[None], "seq", split_axis=3, concat_axis=0, tiled=True),
-    )
+    lane = jnp.arange(ADIM)
+    marks = jnp.where(
+        lane == 0, peak_local[..., None], jnp.where(lane == 1, mass_local[..., None], 0.0)
+    )
+    partials = lax.all_to_all(
+        jnp.stack([summed_local, marks])[None], "seq", split_axis=4, concat_axis=0, tiled=True
+    )
+    pieces = (partials[:, 1, ..., 0], partials[:, 1, ..., 1], partials[:, 0])
     peak_cache = jnp.max(pieces[0], axis=0)
     rescale = jnp.exp(pieces[0] - peak_cache[None])
     mass_cache = jnp.sum(pieces[1] * rescale, axis=0)

time: 299 us -> 272 us (0.910)
  Pallas kernels: 191 us -> 170 us
  waiting for transfers between devices: 0.05 us -> 15.6 us
  starting transfers between devices: 18.6 us -> 8.58 us
  other arithmetic: 29.4 us -> 20.3 us
    pallas_call x1, Pallas kernels: 191 us -> 170 us  [relay_states(): pl.pallas_call(functools.partial(relay_kernel, count, groups), out_shape=...]
    psum x1, waiting for transfers between devices: 0.02 us -> 15.6 us  [on_device(): tails = lax.psum(tails, ('seq', 'grp'))]
    all_to_all x3 -> x1, starting transfers between devices: 15.5 us -> 5.49 us  [on_device(): lax.all_to_all(jnp.stack([summed_local, marks])[None], 'seq', split_axis=...]
    unnamed x71 -> x49, local copies, waits for them, and re-layouts: 7.43 us -> 6.84 us
  transfers between devices with their start and end apart: 5 -> 3, of which waited for: 0 -> 1; matrix products, arithmetic and copies ran while one was open for 21% -> 15% of each run, Pallas kernels for 64% -> 63%
where the time goes in v3:
time: 272 us; the launch traced here: 268 us
  Pallas kernels  170 us (62%)
  local copies, waits for them, and re-layouts  33.2 us (12%)
  other arithmetic  20.3 us (7%)
  waiting for transfers between devices  15.6 us (6%)
  between operations  14.9 us (5%)
  starting transfers between devices  8.58 us (3%)
  matrix products  5.14 us (2%)
    pallas_call x1, Pallas kernels, relay_states(): pl.pallas_call(functools.partial(relay_kernel, count, groups), out_shape=...  170 us
    psum x1, waiting for transfers between devices, on_device(): tails = lax.psum(tails, ('seq', 'grp'))  15.6 us
    unnamed x49, local copies, waits for them, and re-layouts  6.84 us
    all_to_all x1, starting transfers between devices, on_device(): lax.all_to_all(jnp.stack([summed_local, marks])[None], 'seq', split_axis=...  5.49 us
  transfers between devices with their start and end apart: 3, of which 1 were waited for; matrix products, arithmetic and copies ran while one was open for 15% of the time, Pallas kernels for 63%

profile of v3, /device:TPU:25, one launch (start us, length us, event | category | flops | bytes accessed | tf_op | source)
XLA Modules:
  0.0 267.6 jit_solution(12610103263627036173)
XLA Ops:
  7.2 1.8 fusion.77
  9.0 0.3 copy.196
  9.4 0.3 copy-done.19
  9.8 0.8 fusion.81
  10.5 0.5 fusion.34
  11.2 0.3 copy.197
  11.5 0.7 convolution_bitcast_fusion
  12.3 0.3 select_select_fusion
  12.8 1.6 copy.167
  14.4 5.5 %all-to-all-start = ((f32[1,2,2,8,64,128]{5,3,2,1,0,4:T(8,128)}), f32[1,2,2,8,64,128]{5,3,2,1,0,4:T(8,128)}, u32[]{:S(2)}, u32[]{:S(2)}) async-start(f32[1,2,2,8,64,128]{5,3,2,1,0,4:T(8,128)} %copy.167), calls=%async_computation | async-start | bytes 2097152 | tf_op jit(solution)/shard_map/all_to_all | solution.py:575
  20.0 0.8 slice.325
  20.8 0.9 select_dynamic-update-slice_fusion
  21.7 0.7 copy-done.3
  22.5 0.8 dynamic-slice.1
  23.3 0.9 slice_convert_fusion
  24.2 0.6 pad_maximum_fusion.2
  24.8 3.1 %collective-permute-start = (f32[3,5120]{1,0:T(4,128)}, f32[3,5120]{1,0:T(4,128)}, u32[]{:S(2)}, u32[]{:S(2)}) collective-permute-start(f32[3,5120]{1,0:T(4,128)} %pad_maximum_fusion.2), channel_id=1, source_target_pairs={{0,4},{4,8},{8,12},{12,16},{16,20},{20,24},{24,28},{1,5},{5,9},{9,... | collective-permute-start | bytes 184328 | tf_op jit(solution)/shard_map/ppermute | solution.py:31
  28.0 2.5 convert_element_type.47
  30.5 2.5 convert_element_type.48
  33.4 1.2 reduce-window.6
  34.8 0.1 copy_bitcast_fusion.2
  35.4 1.3 fusion.8
  36.8 0.2 slice_reduce_fusion.1
  37.7 0.2 broadcast_in_dim.121
  37.9 0.2 reshape.435
  38.2 0.2 reduce_window_sum.20
  38.4 0.9 constant_dynamic-slice_fusion.6
  39.4 0.5 copy-done.11
  39.9 0.7 mul.566
  40.7 0.7 mul.531
  41.3 0.7 dynamic-slice_reduce_fusion
  42.0 0.8 convolution_bitcast_fusion.1
  42.8 1.7 constant_dynamic-slice_fusion.7
  44.6 0.6 pad.33.clone
  45.2 1.3 dynamic-slice_convert_fusion
  46.5 0.8 maximum_maximum_fusion.rows_ref
  47.3 1.0 constant_dynamic-slice_fusion.5
  48.3 0.7 fusion.80
  49.0 1.6 divide_multiply_fusion
  50.6 2.5 copy.158
  53.1 1.6 copy.159
  54.7 1.6 divide_multiply_fusion.1
  56.3 1.6 copy.157
  57.9 0.2 fusion.10
  58.0 0.6 fusion.25.cb_ref
  58.7 0.2 fusion.9
  58.8 0.9 slice.310
  59.8 169.9 %shard_map.166 = (bf16[512,4096]{1,0:T(8,128)(2,1)}, f32[16,256,128]{2,1,0:T(8,128)S(1)}) custom-call(bf16[512,4096]{1,0:T(8,128)(2,1)} %x_ref.1, f32[8,4096]{1,0:T(8,128)S(1)} %pad.13.lead_ref, f32[8,4096]{1,0:T(8,128)S(1)} %pad.14.taps_ref, f32[32,8,512]{2,1,0:T(8,128)S(1)} %maximum_maximum_fusion.rows_ref, f32[32,8,128]{2,1,0:T(8,128)S(1)} %pad.15.lanes_ref, ...), custom_call_target="tpu_custom_call" | custom-call | tf_op jit(solution)/shard_map/pallas_call | solution.py:377
  229.7 15.6 %all-reduce.6.cloned.1.call-done = f32[3,20480]{1,0:T(4,128)} async-done(((f32[3,20480]{1,0:T(4,128)}), f32[3,20480]{1,0:T(4,128)}) %all-reduce.6.cloned.1.call-update) | async-done | bytes 245776 | tf_op jit(solution)/shard_map/psum | solution.py:449
  245.3 0.8 fusion.79
  246.1 1.0 fusion.72
  247.1 0.2 multiply_reduce_fusion
  248.2 0.6 fusion.4
  248.8 1.1 fusion.61
  250.0 0.6 pad_maximum_fusion.3
  250.6 1.8 copy.229
  252.5 0.3 fusion.78
  252.7 0.8 copy.169
  253.5 0.8 copy.180
  254.5 0.2 fusion.33
  254.8 0.2 copy.178
  255.0 0.4 fusion.51
  255.4 0.6 convert_element_type.57
  256.1 4.7 %copy.235 = bf16[512,4096]{1,0:T(8,128)(2,1)} copy(bf16[512,4096]{1,0:T(8,128)(2,1)} %get-tuple-element.75) | data formatting | bytes 8388608
  (115 shorter events, 4.0 us)
Async XLA Ops:
  7.2 2.6 copy-start
  9.0 0.7 copy-start.19
  12.8 7.1 %copy-start.1 = (bf16[512,2048]{1,0:T(8,128)(2,1)S(1)}, bf16[512,2048]{1,0:T(8,128)(2,1)}, u32[]{:S(2)}) copy-start(bf16[512,2048]{1,0:T(8,128)(2,1)} %param.16) | copy-start | bytes 6291460
  14.4 236.2 %all-to-all-start = ((f32[1,2,2,8,64,128]{5,3,2,1,0,4:T(8,128)}), f32[1,2,2,8,64,128]{5,3,2,1,0,4:T(8,128)}, u32[]{:S(2)}, u32[]{:S(2)}) async-start(f32[1,2,2,8,64,128]{5,3,2,1,0,4:T(8,128)} %copy.167), calls=%async_computation | async-start | bytes 2097152 | tf_op jit(solution)/shard_map/all_to_all | solution.py:575
  19.9 225.4 %all-reduce.6.cloned.1.call-start = ((), (), s32[]{:S(2)}) async-start(), calls=%async_computation.1 | async-start | bytes 655360 | tf_op jit(solution)/shard_map/psum | solution.py:449
  21.7 0.7 copy-start.3
  24.8 23.4 %collective-permute-start = (f32[3,5120]{1,0:T(4,128)}, f32[3,5120]{1,0:T(4,128)}, u32[]{:S(2)}, u32[]{:S(2)}) collective-permute-start(f32[3,5120]{1,0:T(4,128)} %pad_maximum_fusion.2), channel_id=1, source_target_pairs={{0,4},{4,8},{8,12},{12,16},{16,20},{20,24},{24,28},{1,5},{5,9},{9,... | collective-permute-start | bytes 184328 | tf_op jit(solution)/shard_map/ppermute | solution.py:31
  27.9 7.5 %copy-start.17 = (pred[2,2]{1,0:T(4,128)(4,1)}, pred[2,2]{1,0:T(4,128)(4,1)S(1)}, u32[]{:S(2)}) copy-start(pred[2,2]{1,0:T(4,128)(4,1)S(1)} %iota_compare_fusion.1) | copy-start | bytes 16
  28.0 2.6 copy-start.2
  30.5 2.6 copy-start.20
  30.5 2.6 copy-start.4
  33.1 2.1 copy-start.21
  33.1 2.3 copy-start.10
  34.7 4.6 %copy-start.15 = (f32[2,8,32]{2,1,0:T(8,128)S(1)}, f32[2,8,32]{2,1,0:T(8,128)}, u32[]{:S(2)}) copy-start(f32[2,8,32]{2,1,0:T(8,128)} %param.25) | copy-start | bytes 6148
  34.9 6.4 %copy-start.6 = (bf16[2,8,2048]{2,1,0:T(8,128)(2,1)S(1)}, bf16[2,8,2048]{2,1,0:T(8,128)(2,1)}, u32[]{:S(2)}) copy-start(bf16[2,8,2048]{2,1,0:T(8,128)(2,1)} %param.22) | copy-start | bytes 196612
  39.3 0.6 copy-start.11
  59.7 187.4 %copy-start.7 = (f32[2,8,256]{2,1,0:T(8,128)S(1)}, f32[2,8,256]{2,1,0:T(8,128)}, u32[]{:S(2)}) copy-start(f32[2,8,256]{2,1,0:T(8,128)} %get-tuple-element.68) | copy-start | bytes 49156
  59.7 187.4 %copy-start.8 = (f32[2,8,256]{2,1,0:T(8,128)S(1)}, f32[2,8,256]{2,1,0:T(8,128)}, u32[]{:S(2)}) copy-start(f32[2,8,256]{2,1,0:T(8,128)} %get-tuple-element.69) | copy-start | bytes 49156
  59.7 187.6 %copy-start.12 = (f32[2,8,32]{2,1,0:T(8,128)S(1)}, f32[2,8,32]{2,1,0:T(8,128)}, u32[]{:S(2)}) copy-start(f32[2,8,32]{2,1,0:T(8,128)} %copy-done.11) | copy-start | bytes 6148
  59.7 187.6 %copy-start.16 = (f32[2,8,32]{2,1,0:T(8,128)S(1)}, f32[2,8,32]{2,1,0:T(8,128)}, u32[]{:S(2)}) copy-start(f32[2,8,32]{2,1,0:T(8,128)} %param.25) | copy-start | bytes 6148
  229.7 20.2 %copy-start.5 = (f32[1,8,2048]{2,1,0:T(8,128)S(1)}, f32[1,8,2048]{2,1,0:T(8,128)}, u32[]{:S(2)}) copy-start(f32[1,8,2048]{2,1,0:T(8,128)} %mul.566) | copy-start | bytes 196612
  229.7 20.2 %copy-start.13 = (f32[2048]{0:T(1024)S(1)}, f32[2048]{0:T(1024)}, u32[]{:S(2)}) copy-start(f32[2048]{0:T(1024)} %mul.531) | copy-start | bytes 24580
  252.4 1.9 copy-start.14
  252.4 1.9 copy-start.18
  252.5 2.5 copy-start.9
Sparse Core Ops, SparseCore 0:
  26.1 219.1 all-reduce.5
